TPU v7x, 32 devices: a whole 2x2x4 slice. The times are simulated.
32 devices in a mesh: frame: 4 (over y, x), head: 4 (over z), dp: 2 (over core).
Axes of the slice: x: 2, y: 2, z: 4, core: 2. Of those that a mesh axis runs over, the one named last changes fastest.
Arguments:
- latent: bfloat16 [16, 8, 24, 5120], P(('dp', 'frame'), 'head'), parts along dimension 0, may hold values from -6 to 6, as said below
- pose_maps: bfloat16 [16, 16, 48, 256], P(('dp', 'frame'), 'head'), parts along dimension 0, may hold values from -6 to 6
- conv_weight: bfloat16 [3, 3, 3, 256, 320], replicated, may hold values from -0.078125 to 0.078125
- conv_bias: float32 [320], replicated, may hold values from -3 to 3
- pose_proj: bfloat16 [320, 5120], replicated, may hold values from -0.3125 to 0.3125
- w_qkv: bfloat16 [5120, 20, 3, 128], P('frame', 'head'), may hold values from -2 to 2
- w_out: bfloat16 [20, 128, 5120], P('head'), may hold values from -1 to 1
- clip_lengths: int32 [6], P('dp'), parts along dimension 0, may hold values from 1 to 4, 8 in all
- block_ids: int32 [16], P('dp'), parts along dimension 0, may hold values from 0 to 3, never falling along the last dimension, each value on 1 to 3 neighbouring positions
Outputs:
- attended: bfloat16 [16, 8, 24, 5120], P(('dp', 'frame'), 'head'), parts along dimension 0
There are 2 independent parts, one for each index of `dp`. A program takes and returns all parts, laid end to end along the dimension named above; an argument that names none is the same for every part. Nothing has to cross between parts.
Inputs may be any that keep to these rules, and one draw needn't show every extreme that they name: `clip_lengths`: the clips together cover all 8 frames; the longest clip has exactly 4 frames. `block_ids`: never falls along the frames; every block id in the range is used, by at most 3 consecutive frames. `latent`: activations of order one.
All inputs are finite; a program needn't handle non-finite values.
Results may differ from a plain program's by a relative error of at most 0.017.
Values may be sent and summed in bfloat16 or wider, within the bound.
No kernel may reach another device: no remote copies, remote signals or barrier semaphores. Data moves between devices by JAX's collectives and lax.ppermute only.
A program may use at most 128 MiB of HBM per device.

v0:
```python
import jax
import jax.numpy as jnp
from jax import lax
from jax.experimental import pallas as pl
from jax.experimental.pallas import tpu as pltpu
from jax.sharding import PartitionSpec as P

NEG_FILL = -1e30
MIB = 1 << 20
F32 = jnp.float32
BF16 = jnp.bfloat16
PLANE = 4
FIRST_COLUMNS = 8


def cost(flops, moved, exps=0):
    return pl.CostEstimate(flops=int(flops), bytes_accessed=int(moved), transcendentals=int(exps))


def shifted(value, axis, steps):
    count = lax.axis_size(axis)
    leading, last = (max(0, -steps), min(count, count - steps))
    return lax.ppermute(value, axis, [(source, source + steps) for source in range(leading, last)])


def frame_tables(clip_lengths, frame_count):
    clip_ends = jnp.cumsum(clip_lengths)
    clip_starts = clip_ends - clip_lengths
    frame_index = jnp.arange(frame_count, dtype=jnp.int32)
    clip_of = jnp.sum((frame_index[:, None] >= clip_ends[None, :]).astype(jnp.int32), axis=1)
    clip_match = clip_of[:, None] == jnp.arange(clip_lengths.shape[0], dtype=jnp.int32)[None, :]
    start_of = jnp.sum(jnp.where(clip_match, clip_starts[None, :], 0), axis=1)
    return (clip_of, start_of)


def guide_features(latent, pose_maps, conv_weight, conv_bias, pose_proj, start_of, first_frame):
    frames_dev = pose_maps.shape[0]
    upper_row = shifted(pose_maps[:, -1:], "head", 1)
    rows_ext = jnp.concatenate([upper_row, pose_maps], axis=1)
    left_column = jnp.zeros(rows_ext.shape[:2] + (1, rows_ext.shape[3]), rows_ext.dtype)
    cols_ext = jnp.concatenate([left_column, rows_ext], axis=2)
    earlier = shifted(cols_ext, "frame", 1)
    extended = jnp.concatenate([earlier, cols_ext], axis=0)
    out_rows = pose_maps.shape[1] // 2
    out_cols = pose_maps.shape[2] // 2
    frame_ids = first_frame + jnp.arange(frames_dev, dtype=jnp.int32)
    starts_here = lax.dynamic_slice_in_dim(start_of, first_frame, frames_dev)
    tap_list = []
    for step_a in range(3):
        keep_mask = (frame_ids - 2 + step_a >= starts_here).astype(pose_maps.dtype)[
            :, None, None, None
        ]
        frames_tap = extended[step_a : step_a + frames_dev] * keep_mask
        for step_b in range(3):
            for step_e in range(3):
                tap_list.append(
                    frames_tap[
                        :,
                        step_b : step_b + 2 * out_rows - 1 : 2,
                        step_e : step_e + 2 * out_cols - 1 : 2,
                    ]
                )
    stacked = jnp.concatenate(tap_list, axis=3)
    kernel = conv_weight.reshape(-1, conv_weight.shape[-1])
    summed = jnp.dot(stacked, kernel, preferred_element_type=jnp.float32) + conv_bias
    feature = jax.nn.silu(summed).astype(jnp.bfloat16)
    guided = latent.astype(jnp.float32) + jnp.dot(
        feature, pose_proj, preferred_element_type=jnp.float32
    )
    return guided.astype(jnp.bfloat16)


def attend_rows(queries, query_clip, query_block, keyvals, clip_of, block_ids):
    heads_dev = queries.shape[1]
    rows_query = queries.shape[0]
    head_size = queries.shape[2]
    score_scale = head_size ** (-0.5)
    start_carry = (
        jnp.full((heads_dev, rows_query), NEG_FILL, jnp.float32),
        jnp.zeros((heads_dev, rows_query), jnp.float32),
        jnp.zeros((heads_dev, rows_query, head_size), jnp.float32),
    )

    def one_frame(running, frame_item):
        frame_kv, frame_id = frame_item
        key_clip = clip_of[frame_id]
        key_block = block_ids[frame_id]
        visible = (query_clip == key_clip) & (key_block <= query_block)
        run_max, run_total, run_acc = running
        scores = (
            jnp.einsum(
                "qhd,khd->hqk", queries, frame_kv[:, :, 0], preferred_element_type=jnp.float32
            )
            * score_scale
        )
        scores = jnp.where(visible[None, :, None], scores, NEG_FILL)
        new_max = jnp.maximum(run_max, jnp.max(scores, axis=2))
        factor = jnp.exp(run_max - new_max)
        weights = jnp.where(visible[None, :, None], jnp.exp(scores - new_max[:, :, None]), 0.0)
        new_total = run_total * factor + jnp.sum(weights, axis=2)
        new_acc = run_acc * factor[:, :, None] + jnp.einsum(
            "hqk,khd->hqd",
            weights.astype(jnp.bfloat16),
            frame_kv[:, :, 1],
            preferred_element_type=jnp.float32,
        )
        running = (new_max, new_total, new_acc)
        return (running, None)

    running = start_carry
    shard_piece = lax.all_gather(keyvals, "frame", axis=0, tiled=True)
    piece_frames = shard_piece.shape[0]
    frame_list = jnp.arange(piece_frames, dtype=jnp.int32)
    running, unused = lax.scan(one_frame, running, (shard_piece, frame_list))
    run_max, run_total, run_acc = running
    normalized = run_acc / run_total[:, :, None]
    return jnp.transpose(normalized, (1, 0, 2)).astype(jnp.bfloat16)


def plain_shards(
    latent, pose_maps, conv_weight, conv_bias, pose_proj, w_qkv, w_out, clip_lengths, block_ids
):
    frame_count = block_ids.shape[0]
    clip_of, start_of = frame_tables(clip_lengths, frame_count)
    frames_dev = latent.shape[0]
    first_frame = lax.axis_index("frame") * frames_dev
    guided = guide_features(
        latent, pose_maps, conv_weight, conv_bias, pose_proj, start_of, first_frame
    )
    whole_rows = lax.all_gather(guided, "head", axis=1, tiled=True)
    height = whole_rows.shape[1]
    width_grid = whole_rows.shape[2]
    model_width = whole_rows.shape[3]
    flat_tokens = whole_rows.reshape(-1, model_width)
    qkv_local = w_qkv.reshape(w_qkv.shape[0], -1)
    projected = jnp.dot(
        flat_tokens,
        lax.all_gather(qkv_local, "frame", axis=0, tiled=True),
        preferred_element_type=jnp.float32,
    ).astype(jnp.bfloat16)
    per_frame = height * width_grid
    heads_dev = w_qkv.shape[1]
    head_size = w_qkv.shape[3]
    grouped = projected.reshape(frames_dev, per_frame, heads_dev, 3, head_size)
    rows_total = frames_dev * per_frame
    queries = grouped[:, :, :, 0].reshape(rows_total, heads_dev, head_size)
    keyvals = grouped[:, :, :, 1:3]
    clip_rows = lax.dynamic_slice_in_dim(clip_of, first_frame, frames_dev)
    block_rows = lax.dynamic_slice_in_dim(block_ids, first_frame, frames_dev)
    query_clip = jnp.repeat(clip_rows, per_frame)
    query_block = jnp.repeat(block_rows, per_frame)
    attended = attend_rows(queries, query_clip, query_block, keyvals, clip_of, block_ids)
    by_row = attended.reshape(frames_dev, height, width_grid, heads_dev * head_size)
    by_row = jnp.transpose(by_row, (1, 0, 2, 3)).reshape(
        height, frames_dev * width_grid, heads_dev * head_size
    )
    out_weight = w_out.reshape(heads_dev * head_size, w_out.shape[2])
    rows_here = height // lax.axis_size("head")
    summed_rows = lax.psum_scatter(
        jnp.dot(by_row, out_weight, preferred_element_type=jnp.float32).astype(jnp.bfloat16),
        "head",
        scatter_dimension=0,
        tiled=True,
    ).astype(jnp.float32)
    summed_rows = summed_rows.reshape(rows_here, frames_dev, width_grid, out_weight.shape[1])
    return jnp.transpose(summed_rows, (1, 0, 2, 3)).astype(jnp.bfloat16)


def turn(value, axis, steps):
    count = lax.axis_size(axis)
    return lax.ppermute(value, axis, [(i, (i + steps) % count) for i in range(count)])


def across(value, axis, bits):
    count = lax.axis_size(axis)
    return lax.ppermute(value, axis, [(i, i ^ bits) for i in range(count)])


def hop(lower, upper, axis, s):
    count = lax.axis_size(axis)
    lower = lax.ppermute(lower, axis, [(i, i + 1) for i in range(s - 1, count - 1)])
    upper = lax.ppermute(upper, axis, [(i, i - 1) for i in range(1, count - s + 1)])
    return lower, upper


def after(value, *others):
    def body(*refs):
        del refs

    anywhere = pl.BlockSpec(memory_space=pl.ANY)
    return pl.pallas_call(
        body,
        out_shape=jax.ShapeDtypeStruct(value.shape, value.dtype),
        in_specs=[anywhere] * (1 + len(others)),
        out_specs=anywhere,
        input_output_aliases={0: 0},
        name="after",
    )(value, *others)


def take_block(weight, row, column, shape, *ready):
    def body(at_ref, weight_ref, *refs):
        refs[-1][...] = weight_ref[...]

    return pl.pallas_call(
        body,
        out_shape=jax.ShapeDtypeStruct(shape, weight.dtype),
        grid_spec=pltpu.PrefetchScalarGridSpec(
            num_scalar_prefetch=1,
            grid=(1,),
            in_specs=[pl.BlockSpec(shape, lambda i, at: (at[0], at[1]))]
            + [pl.BlockSpec(memory_space=pl.ANY)] * len(ready),
            out_specs=pl.BlockSpec(shape, lambda i, at: (0, 0)),
        ),
        cost_estimate=cost(0, 4 * shape[0] * shape[1]),
        name="take_block",
    )(jnp.stack([row, column]), weight, *ready)


def conv_kernel(keep_ref, cols_ref, weight_ref, bias_ref, out_ref, acc_ref):
    step = pl.program_id(0)
    tap_a, tap_b = step // 3, step % 3
    frames, strip_rows, width = out_ref.shape[0], out_ref.shape[1], cols_ref.shape[2]
    pieces = []
    for t in range(frames):
        keep = keep_ref[tap_a * frames + t]
        for r in range(strip_rows):
            rows = cols_ref[tap_a + t, tap_b + 2 * r].astype(F32)
            pieces.append(jnp.where(keep > 0, rows, 0.0))
    lhs = jnp.concatenate(pieces, axis=0).astype(BF16)
    channels = weight_ref.shape[3]
    total = None
    for e in range(3):
        part = lax.dot_general(
            lhs[:, e * channels : (e + 1) * channels],
            weight_ref[0, e],
            (((1,), (1,)), ((), ())),
            preferred_element_type=F32,
        )
        total = part if total is None else total + part

    @pl.when(step == 0)
    def _():
        acc_ref[...] = total

    @pl.when(step > 0)
    def _():
        acc_ref[...] += total

    @pl.when(step == 8)
    def _():
        summed = acc_ref[...] + bias_ref[...]
        feature = summed / (1.0 + jnp.exp(-summed))
        for t in range(frames):
            for r in range(strip_rows):
                at = (t * strip_rows + r) * width
                out_ref[t, r] = feature[at : at + width].astype(BF16)


def pose_feature(extended, conv_weight, conv_bias, start_of, first_frame):
    frames, rows, columns, channels = extended.shape
    frames, rows = frames // 2, rows - 1
    out_channels = conv_weight.shape[-1]
    pairs = extended.reshape(2 * frames, rows + 1, columns // 2, 2 * channels)
    before = jnp.pad(pairs[:, :, :-1, channels:], ((0, 0), (0, 0), (1, 0), (0, 0)))
    cols = jnp.concatenate([before, pairs], axis=3)
    taps = jnp.transpose(conv_weight, (0, 1, 2, 4, 3)).reshape(9, 3, out_channels, channels)
    frame_ids = first_frame + jnp.arange(frames, dtype=jnp.int32)
    starts_here = lax.dynamic_slice_in_dim(start_of, first_frame, frames)
    keep = (frame_ids[None, :] - 2 + jnp.arange(3, dtype=jnp.int32)[:, None] >= starts_here[None, :])
    keep = keep.astype(jnp.int32).reshape(-1)
    out_shape = (frames, rows // 2, columns // 2, out_channels)
    tokens = frames * (rows // 2) * (columns // 2)
    feature = pl.pallas_call(
        conv_kernel,
        out_shape=jax.ShapeDtypeStruct(out_shape, BF16),
        grid_spec=pltpu.PrefetchScalarGridSpec(
            num_scalar_prefetch=1,
            grid=(9,),
            in_specs=[
                pl.BlockSpec(cols.shape, lambda i, k: (0, 0, 0, 0)),
                pl.BlockSpec((1, 3, out_channels, channels), lambda i, k: (i, 0, 0, 0)),
                pl.BlockSpec((1, out_channels), lambda i, k: (0, 0)),
            ],
            out_specs=pl.BlockSpec(out_shape, lambda i, k: (0, 0, 0, 0)),
            scratch_shapes=[pltpu.VMEM((tokens, out_channels), F32)],
        ),
        compiler_params=pltpu.CompilerParams(vmem_limit_bytes=24 * MIB),
        cost_estimate=cost(tokens * out_channels, 2 * tokens * out_channels),
        name="pose_conv",
    )(keep, cols, taps, conv_bias.reshape(1, -1))
    return feature.reshape(tokens, out_channels)


def project(own, lower, upper, features, pose_proj, order, shards_of, total, frames):
    strips = len(features)
    tokens = own.shape[0]
    channels = pose_proj.shape[0]
    rows = strips * tokens
    per_frame = tokens // frames
    steps = len(shards_of)
    flat = [array for kind, arrays in shards_of for array in arrays]
    size = flat[0].shape[2]
    columns = 3 * (PLANE + 1)
    heads = PLANE + 1
    depth = own.shape[1] // PLANE
    cuts = [(c, min(c + 4, columns)) for c in range(0, columns, 4)]
    parts = 2 if shards_of[0][0] == "rows" else 1
    slots = min(2, steps)

    def body(order_ref, *refs):
        own_ref, lower_refs, upper_refs = refs[0], refs[1:strips], refs[strips : 2 * strips - 1]
        feature_refs = refs[2 * strips - 1 : 3 * strips - 1]
        proj_ref = refs[3 * strips - 1]
        source_refs = refs[3 * strips : 3 * strips + len(flat)]
        rest = refs[3 * strips + len(flat) :]
        held_ref, guided_ref, sems = rest[-3:]
        if total is None:
            sum_ref = rest[0]
        else:
            total_ref, last_ref, sum_ref = rest[0], rest[1 + PLANE], rest[2 + PLANE]
            message_refs = rest[1 : 1 + PLANE]
        step = pl.program_id(0)

        def fetch(k, n, part):
            low, high = cuts[n]
            kind, arrays = shards_of[k]
            base = sum(len(other) for unused, other in shards_of[:k])
            length, at, shift = depth // parts, 0, 0
            if kind != "whole" and low >= FIRST_COLUMNS:
                base, shift = base + 1, FIRST_COLUMNS
            if kind == "rows":
                base += 2 * part
                at = pl.multiple_of((order_ref[steps + 1] ^ part) * length, 128)
            return pltpu.make_async_copy(
                source_refs[base].at[low - shift : high - shift],
                held_ref.at[k % slots, low:high, pl.ds(at, length)],
                sems.at[k % slots, n, part],
            )

        def start(k):
            for n in range(len(cuts)):
                for part in range(parts):
                    fetch(k, n, part).start()

        for k in range(steps):

            @pl.when(step == max(k - 1, 0))
            def _(k=k):
                start(k)

        feature = jnp.concatenate([ref[...] for ref in feature_refs], axis=0)
        added = jnp.dot(feature, proj_ref[...], preferred_element_type=F32)
        for s in range(strips):
            latent = own_ref[...].astype(F32)
            if s > 0:
                latent = lower_refs[s - 1][...].astype(F32) + upper_refs[strips - s - 1][...].astype(F32)
            guided = (latent + added[s * tokens : (s + 1) * tokens]).astype(BF16)
            for t in range(frames):
                at = (t * strips + s) * per_frame
                guided_ref[at : at + per_frame] = guided[t * per_frame : (t + 1) * per_frame]

        slot = lax.rem(step, slots)
        for n, (low, high) in enumerate(cuts):
            for k in range(steps):

                @pl.when(step == k)
                def _(k=k, n=n):
                    for part in range(parts):
                        fetch(k, n, part).wait()

            rhs = jnp.concatenate([held_ref[slot, c] for c in range(low, high)], axis=1)
            part = jnp.dot(guided_ref[...], rhs, preferred_element_type=F32)
            lanes = slice(low * size, high * size)
            if total is not None:
                sum_ref[:, lanes] = total_ref[:, lanes] + part
                continue

            @pl.when(step == 0)
            def _(lanes=lanes, part=part):
                sum_ref[:, lanes] = part

            @pl.when(step > 0)
            def _(lanes=lanes, part=part):
                sum_ref[:, lanes] += part

        if total is None:
            return
        last = 3 * (heads - 1) * size
        last_ref[...] = sum_ref[:, last : last + size].astype(BF16)
        for r in range(PLANE):
            head = order_ref[steps] ^ r
            for j in range(3):
                at = pl.multiple_of((3 * head + j) * size, size)
                message_refs[r][j] = sum_ref[:, pl.ds(at, size)].astype(BF16)
            for j in range(1, 3):
                at = last + j * size
                message_refs[r][2 + j] = sum_ref[:, at : at + size].astype(BF16)

    piece = pl.BlockSpec((tokens, depth), lambda i, order: (0, order[i]))
    in_specs = [piece] * (2 * strips - 1)
    in_specs += [pl.BlockSpec((tokens, channels), lambda i, order: (0, 0))] * strips
    in_specs += [pl.BlockSpec((channels, depth), lambda i, order: (0, order[i]))]
    in_specs += [pl.BlockSpec(memory_space=pl.ANY)] * len(flat)
    operands = [own, *lower, *upper, *features, pose_proj, *flat]
    sums = pl.BlockSpec((rows, columns * size), lambda i, order: (0, 0))
    scratch = [
        pltpu.VMEM((slots, columns, depth, size), BF16),
        pltpu.VMEM((rows, depth), BF16),
        pltpu.SemaphoreType.DMA((slots, len(cuts), parts)),
    ]
    if total is None:
        out_shape, out_specs = jax.ShapeDtypeStruct((rows, columns * size), F32), sums
    else:
        assert steps == 1
        in_specs.append(sums)
        operands.append(total)
        message = jax.ShapeDtypeStruct((5, rows, size), BF16)
        out_shape = (message,) * PLANE + (jax.ShapeDtypeStruct((rows, size), BF16),)
        out_specs = (pl.BlockSpec((5, rows, size), lambda i, order: (0, 0, 0)),) * PLANE
        out_specs += (pl.BlockSpec((rows, size), lambda i, order: (0, 0)),)
        scratch = [pltpu.VMEM((rows, columns * size), F32)] + scratch
    return pl.pallas_call(
        body,
        out_shape=out_shape,
        grid_spec=pltpu.PrefetchScalarGridSpec(
            num_scalar_prefetch=1, grid=(steps,), in_specs=in_specs, out_specs=out_specs, scratch_shapes=scratch
        ),
        compiler_params=pltpu.CompilerParams(vmem_limit_bytes=40 * MIB),
        cost_estimate=cost(0, 2 * rows * size),
        name="project",
    )(order, *operands)


def attend(messages, last_query, here, spans, frames, strips):
    rows, size = last_query.shape
    per_frame = rows // frames
    strip = per_frame // strips
    frame_count = PLANE * frames
    window = frame_count - 4 if frame_count > 4 else frame_count
    out_rows = (PLANE + 1) * frames * strip
    scale = size ** (-0.5)

    def body(table_ref, *refs):
        message_refs, last_ref = refs[:PLANE], refs[PLANE]
        out_refs, held_ref = refs[PLANE + 1 : PLANE + 1 + strips], refs[-1]
        here_at = table_ref[3 * frame_count]
        for r in range(PLANE):
            for t in range(frames):
                frame = (here_at ^ r) * frames + t
                for j in range(4):
                    held_ref[frame, j] = message_refs[r][j + 1, t * per_frame : (t + 1) * per_frame]

        def one(query, frame, kind, at):
            begin, low, high = table_ref[3 * frame], table_ref[3 * frame + 1], table_ref[3 * frame + 2]
            keys = held_ref[pl.ds(begin, window), kind].reshape(window * per_frame, size)
            values = held_ref[pl.ds(begin, window), kind + 1].reshape(window * per_frame, size)
            scores = lax.dot_general(query, keys, (((1,), (1,)), ((), ())), preferred_element_type=F32)
            place = lax.broadcasted_iota(jnp.int32, (1, window * per_frame), 1)
            seen = (place >= low * per_frame) & (place < high * per_frame)
            scores = jnp.where(seen, scores * scale, NEG_FILL)
            weights = jnp.exp(scores - jnp.max(scores, axis=1, keepdims=True))
            totals = jnp.sum(weights, axis=1, keepdims=True)
            mixed = jnp.dot(weights.astype(BF16), values, preferred_element_type=F32)
            result = (mixed / totals).astype(BF16)
            for s in range(strips):
                out_refs[s][at : at + strip] = result[s * strip : (s + 1) * strip]

        for r in range(PLANE):
            for t in range(frames):
                query = message_refs[r][0, t * per_frame : (t + 1) * per_frame]
                one(query, (here_at ^ r) * frames + t, 0, (r * frames + t) * strip)
        for t in range(frames):
            query = last_ref[t * per_frame : (t + 1) * per_frame]
            one(query, here_at * frames + t, 2, (PLANE * frames + t) * strip)

    table = jnp.concatenate([spans.reshape(-1), here.reshape(1)]).astype(jnp.int32)
    whole = pl.BlockSpec((5, rows, size), lambda i, table: (0, 0, 0))
    units = (PLANE + 1) * frames
    return pl.pallas_call(
        body,
        out_shape=(jax.ShapeDtypeStruct((out_rows, size), BF16),) * strips,
        grid_spec=pltpu.PrefetchScalarGridSpec(
            num_scalar_prefetch=1,
            grid=(1,),
            in_specs=[whole] * PLANE + [pl.BlockSpec((rows, size), lambda i, table: (0, 0))],
            out_specs=(pl.BlockSpec((out_rows, size), lambda i, table: (0, 0)),) * strips,
            scratch_shapes=[pltpu.VMEM((frame_count, 4, per_frame, size), BF16)],
        ),
        compiler_params=pltpu.CompilerParams(vmem_limit_bytes=40 * MIB),
        cost_estimate=cost(0, 2 * rows * size),
        name="attend",
    )(table, *messages, last_query)


def out_project(gathered, weights, here, group, core, tokens):
    groups, depth, columns = weights[0].shape
    size = gathered[0].shape[2]
    heads = depth // size

    def body(at_ref, *refs):
        weight_refs = refs[PLANE : PLANE + 2]
        out_refs, lhs_ref, sum_ref = refs[PLANE + 2 : -2], refs[-2], refs[-1]
        step = pl.program_id(0)
        for p in range(PLANE):
            rows = slice(p * tokens, (p + 1) * tokens)
            for q in range(PLANE):
                at = (p ^ q) * tokens
                lhs_ref[rows, q * size : (q + 1) * size] = refs[q][0, at : at + tokens]
            lhs_ref[rows, PLANE * size :] = refs[p][0, PLANE * tokens :]

        here_at, core_at = at_ref[0], at_ref[2]
        for c in range(2):
            found = [
                weight_refs[c][0, pl.ds(pl.multiple_of((here_at ^ q) * size, size), size)] for q in range(PLANE)
            ]
            found.append(weight_refs[c][0, PLANE * size : heads * size])
            part = jnp.dot(lhs_ref[...], jnp.concatenate(found, axis=0), preferred_element_type=F32)
            part = part.astype(BF16).astype(F32)

            @pl.when(step == 0)
            def _(c=c, part=part):
                sum_ref[c] = part

            @pl.when(step > 0)
            def _(c=c, part=part):
                sum_ref[c] += part

        @pl.when(step == groups - 1)
        def _():
            for p in range(PLANE):
                for c in range(2):
                    at = pl.multiple_of((core_at ^ c) * columns, 128)
                    out_refs[p][:, pl.ds(at, columns)] = sum_ref[c, p * tokens : (p + 1) * tokens].astype(BF16)

    in_specs = [pl.BlockSpec((1,) + piece.shape[1:], lambda g, at: (g, 0, 0)) for piece in gathered]
    in_specs += [
        pl.BlockSpec((1, depth, columns), lambda g, at: (lax.rem(at[1] + g, groups), 0, 0))
    ] * 2
    return pl.pallas_call(
        body,
        out_shape=(jax.ShapeDtypeStruct((tokens, 2 * columns), BF16),) * PLANE,
        grid_spec=pltpu.PrefetchScalarGridSpec(
            num_scalar_prefetch=1,
            grid=(groups,),
            in_specs=in_specs,
            out_specs=(pl.BlockSpec((tokens, 2 * columns), lambda g, at: (0, 0)),) * PLANE,
            scratch_shapes=[
                pltpu.VMEM((PLANE * tokens, depth), BF16),
                pltpu.VMEM((2, PLANE * tokens, columns), F32),
            ],
        ),
        compiler_params=pltpu.CompilerParams(vmem_limit_bytes=24 * MIB),
        cost_estimate=cost(0, 4 * PLANE * tokens * columns),
        name="out_project",
    )(jnp.stack([here, group, core]), *gathered, *weights)


def place_columns(pieces, here):
    tokens, columns = pieces[0].shape

    def body(here_ref, *refs):
        for r in range(PLANE):
            at = pl.multiple_of((here_ref[0] ^ r) * columns, 128)
            refs[-1][:, pl.ds(at, columns)] = refs[r][...]

    return pl.pallas_call(
        body,
        out_shape=jax.ShapeDtypeStruct((tokens, PLANE * columns), BF16),
        grid_spec=pltpu.PrefetchScalarGridSpec(
            num_scalar_prefetch=1,
            grid=(1,),
            in_specs=[pl.BlockSpec((tokens, columns), lambda i, here: (0, 0))] * PLANE,
            out_specs=pl.BlockSpec((tokens, PLANE * columns), lambda i, here: (0, 0)),
        ),
        cost_estimate=cost(0, 4 * tokens * PLANE * columns),
        name="place_columns",
    )(here.reshape(1), *pieces)


def shards(
    latent, pose_maps, conv_weight, conv_bias, pose_proj, w_qkv, w_out, clip_lengths, block_ids
):
    frame_count = block_ids.shape[0]
    frames, strip_rows, width_grid, model_width = latent.shape
    heads, head_size = w_qkv.shape[1], w_qkv.shape[3]
    strips = lax.axis_size("head")
    tokens = frames * strip_rows * width_grid
    here = lax.axis_index("frame").astype(jnp.int32)
    group = lax.axis_index("head").astype(jnp.int32)
    core = lax.axis_index("dp").astype(jnp.int32)
    clip_of, start_of = frame_tables(clip_lengths, frame_count)

    weight = jnp.transpose(w_qkv, (1, 2, 0, 3)).reshape(3 * heads, -1, head_size)
    near_pairs = [(2 * f + c, 2 * (f ^ (1 + c)) + c) for f in range(PLANE) for c in range(2)]
    far_pairs = [(2 * f + c, 2 * (f ^ (2 - c)) + c) for f in range(PLANE) for c in range(2)]
    plane_axes = ("frame", "dp")
    near_first = lax.ppermute(weight[:FIRST_COLUMNS], plane_axes, near_pairs)
    near_rest = weight[FIRST_COLUMNS:]
    earlier = shifted(after(pose_maps, near_rest), "frame", 1)

    own = latent.reshape(tokens, model_width)
    lower, upper = hop(own, own, "head", 1)
    lower, upper = [lower], [upper]
    lower[0], upper[0] = after(lower[0], earlier), after(upper[0], earlier)
    near_rest = after(near_rest, near_first, lower[0], upper[0])
    near_rest = lax.ppermute(near_rest, plane_axes, near_pairs)
    extended = jnp.concatenate([earlier, pose_maps], axis=0)
    rows_above = shifted(extended[:, -1:], "head", 1)
    extended = jnp.concatenate([rows_above, extended], axis=1)

    columns = model_width // PLANE // 2
    depth = heads * head_size
    out_half = take_block(w_out.reshape(depth, model_width), jnp.int32(0), 2 * here + core, (depth, columns))

    for s in range(2, strips):
        below, above = hop(lower[-1], upper[-1], "head", s)
        if s < strips - 1:
            below, above = after(below, rows_above), after(above, rows_above)
        lower.append(below)
        upper.append(above)
    start_of = after(start_of, lower[1], upper[1], out_half)
    feature = pose_feature(extended, conv_weight, conv_bias, start_of, here * frames)
    half_rows = weight.shape[1] // 2
    first_half = lax.dynamic_slice_in_dim(near_first, core * half_rows, half_rows, axis=1)
    first_half = after(first_half, lower[1])
    near_rest = after(near_rest, lower[1], upper[1], first_half)
    near = (near_first, near_rest)
    rest_half = lax.dynamic_slice_in_dim(near_rest, core * half_rows, half_rows, axis=1)
    rest_half = after(rest_half, feature)
    far = tuple(lax.ppermute(part, plane_axes, far_pairs) for part in (first_half, rest_half))
    feature = after(feature, near_rest)
    features = [feature] + [turn(feature, "head", s) for s in range(1, strips)]
    other = tuple(across(part, "dp", 1) for part in near)
    out_half = after(out_half, lower[-1], upper[-1], *features[1:])

    here_near, here_other, here_far = here ^ (1 + core), here ^ (2 - core), here ^ 3
    order = after(jnp.stack([here, here_near, here_other, here, core]), out_half)
    held = [("whole", (weight,)), ("columns", near), ("columns", other)]
    total = project(own, lower, upper, features, pose_proj, order, held, None, frames)
    far = tuple(after(part, total) for part in far)
    far += tuple(across(part, "dp", 1) for part in far)
    order = jnp.stack([here_far, here, core])
    *messages, last_query = project(
        own, lower, upper, features, pose_proj, order, [("rows", far)], total, frames
    )
    messages = [messages[0]] + [across(messages[r], "frame", r) for r in range(1, PLANE)]

    same_clip = clip_of[:, None] == clip_of[None, :]
    counts = jnp.sum((same_clip & (block_ids[None, :] <= block_ids[:, None])).astype(jnp.int32), axis=1)
    window = frame_count - 4 if frame_count > 4 else frame_count
    begins = jnp.minimum(start_of, frame_count - window)
    spans = jnp.stack([begins, start_of - begins, start_of - begins + counts], axis=1)
    outs = attend(messages, last_query, here, spans, frames, strips)

    out_half = after(lax.all_gather(out_half, "head"), outs[0])
    out_weights = [out_half, across(out_half, "dp", 1)]

    strip_heads = [outs[0]] + [turn(outs[s], "head", -s) for s in range(1, strips)]
    strip_heads = jnp.stack(strip_heads)
    gathered = [strip_heads] + [across(strip_heads, "frame", r) for r in range(1, PLANE)]
    done = out_project(gathered, out_weights, here, group, core, tokens)
    mine = [done[0]] + [across(done[r], "frame", r) for r in range(1, PLANE)]
    return place_columns(mine, here).reshape(latent.shape)


def solution(mesh):
    return jax.shard_map(
        shards if mesh.shape["frame"] == PLANE else plain_shards,
        mesh=mesh,
        in_specs=(
            P(("dp", "frame"), "head", None, None),
            P(("dp", "frame"), "head", None, None),
            P(),
            P(),
            P(),
            P("frame", "head", None, None),
            P("head", None, None),
            P("dp"),
            P("dp"),
        ),
        out_specs=P(("dp", "frame"), "head", None, None),
        check_vma=False,
    )
```

profile of v0, /device:TPU:0, one launch (start us, length us, event | category | flops | bytes accessed | tf_op | source)
XLA Modules:
  0.0 252.3 jit_solution(7869790884517597310)
XLA Ops:
  6.5 3.4 %slice.19 = bf16[8,1280,128]{2,1,0:T(8,128)(2,1)} slice(bf16[15,1280,128]{2,1,0:T(8,128)(2,1)} %bitcast.38), slice={[0:8], [0:1280], [0:128]} | slice | bytes 5242880 | tf_op jit(solution)/shard_map/slice | solution.py:598
  9.9 2.9 %collective-permute-start.8 = (bf16[8,1280,128]{2,1,0:T(8,128)(2,1)}, bf16[8,1280,128]{2,1,0:T(8,128)(2,1)S(1)}, u32[]{:S(2)}, u32[]{:S(2)}) collective-permute-start(bf16[8,1280,128]{2,1,0:T(8,128)(2,1)} %slice.19), channel_id=1, source_target_pairs={{0,8},{1,17},{8,0},{9,25},{16,24},{17,1},{24,16},{25,9},{2,10},{3,... | collective-permute-start | bytes 7864328 | tf_op jit(solution)/shard_map/ppermute | solution.py:598
  12.9 4.6 %collective-permute-start = (bf16[96,5120]{1,0:T(8,128)(2,1)}, bf16[96,5120]{1,0:T(8,128)(2,1)}, u32[]{:S(2)}, u32[]{:S(2)}) collective-permute-start(bf16[96,5120]{1,0:T(8,128)(2,1)} %bitcast.5.refs_0_), channel_id=1, source_target_pairs={{0,2},{2,4},{4,6},{1,3},{3,5},{5,7},{8,10},{10,12},{12,14},{9,11},... | collective-permute-start | bytes 2949128 | tf_op jit(solution)/shard_map/ppermute | solution.py:181
  18.7 3.3 %slice.16.refs_1_.refs_0_ = bf16[7,1280,128]{2,1,0:T(8,128)(2,1)} slice(bf16[15,1280,128]{2,1,0:T(8,128)(2,1)} %bitcast.39), slice={[8:15], [0:1280], [0:128]} | slice | bytes 4587520 | tf_op jit(solution)/shard_map/slice | solution.py:599
  22.7 2.4 collective-permute-start.1
  25.1 21.5 %collective-permute-done.1.refs_1_ = bf16[2,4,48,256]{3,2,1,0:T(8,128)(2,1)S(1)} collective-permute-done((bf16[2,4,48,256]{3,2,1,0:T(8,128)(2,1)}, bf16[2,4,48,256]{3,2,1,0:T(8,128)(2,1)S(1)}, u32[]{:S(2)}, u32[]{:S(2)}) %collective-permute-start.1) | collective-permute-done | bytes 196640 | tf_op jit(solution)/shard_map/ppermute | solution.py:23
  48.8 2.4 collective-permute-start.9
  54.5 6.9 %collective-permute-start.3 = (bf16[4,1,48,256]{3,2,1,0:T(8,128)(2,1)S(1)}, bf16[4,1,48,256]{3,2,1,0:T(8,128)(2,1)S(1)}, u32[]{:S(2)}, u32[]{:S(2)}) collective-permute-start(bf16[4,1,48,256]{3,2,1,0:T(8,128)(2,1)S(1)} %slice.17), channel_id=1, source_target_pairs={{0,2},{2,4},{4,6},{1,3},{3,5},{5,7},{8,10},{10,12},{12,14},{9,11},... | collective-permute-start | bytes 294920 | tf_op jit(solution)/shard_map/ppermute | solution.py:23
  66.9 9.0 %collective-permute-done.5.refs_0_ = bf16[96,5120]{1,0:T(8,128)(2,1)} collective-permute-done((bf16[96,5120]{1,0:T(8,128)(2,1)}, bf16[96,5120]{1,0:T(8,128)(2,1)}, u32[]{:S(2)}, u32[]{:S(2)}) %collective-permute-start.5) | collective-permute-done | bytes 983072 | tf_op jit(solution)/shard_map/ppermute | solution.py:182
  77.7 2.9 %take_block.1.refs_3_.refs_0_ = bf16[640,640]{1,0:T(8,128)(2,1)} custom-call(s32[2]{0:T(128)} %pad_add_fusion.1.at_ref, bf16[640,5120]{1,0:T(8,128)(2,1)} %bitcast.41), custom_call_target="tpu_custom_call" | custom-call | bytes 1638400 | tf_op jit(solution)/shard_map/take_block/pallas_call | solution.py:205
  84.6 3.4 %pose_conv.1 = bf16[2,2,24,320]{3,2,1,0:T(8,128)(2,1)S(1)} custom-call(s32[6]{0:T(128)S(1)} %reshape.86.keep_ref, bf16[4,5,24,768]{3,2,1,0:T(8,128)(2,1)S(1)} %fusion.1.cols_ref, bf16[9,3,320,256]{3,2,1,0:T(8,128)(2,1)S(1)} %bitcast.34, f32[1,320]{1,0:T(1,128)S(1)} %reshape.83.bias_ref), custom_call_target="tpu_custom_call" | custom-call | flops 30720 | bytes 61440 | tf_op jit(solution)/shard_map/pose_conv/pallas_call | solution.py:274
  91.1 2.3 constant_dynamic-slice_fusion.refs_0_
  93.5 3.8 %collective-permute-start.10 = (bf16[96,320]{1,0:T(8,128)(2,1)}, bf16[96,320]{1,0:T(8,128)(2,1)S(1)}, u32[]{:S(2)}, u32[]{:S(2)}) collective-permute-start(bf16[96,320]{1,0:T(8,128)(2,1)} %after.25.refs_7_), channel_id=1, source_target_pairs={{0,2},{2,4},{4,6},{6,0},{1,3},{3,5},{5,7},{7,1},{8,10},{10,12},{12... | collective-permute-start | bytes 184328 | tf_op jit(solution)/shard_map/ppermute | solution.py:171
  97.2 4.2 %collective-permute-start.11 = (bf16[96,320]{1,0:T(8,128)(2,1)}, bf16[96,320]{1,0:T(8,128)(2,1)S(1)}, u32[]{:S(2)}, u32[]{:S(2)}) collective-permute-start(bf16[96,320]{1,0:T(8,128)(2,1)} %after.25.refs_7_), channel_id=1, source_target_pairs={{0,4},{2,6},{4,0},{6,2},{1,5},{3,7},{5,1},{7,3},{8,12},{10,14},{12... | collective-permute-start | bytes 184328 | tf_op jit(solution)/shard_map/ppermute | solution.py:171
  101.4 2.8 %collective-permute-start.12 = (bf16[96,320]{1,0:T(8,128)(2,1)}, bf16[96,320]{1,0:T(8,128)(2,1)}, u32[]{:S(2)}, u32[]{:S(2)}) collective-permute-start(bf16[96,320]{1,0:T(8,128)(2,1)} %after.25.refs_7_), channel_id=1, source_target_pairs={{0,6},{2,0},{4,2},{6,4},{1,7},{3,1},{5,3},{7,5},{8,14},{10,8},{12,... | collective-permute-start | bytes 184328 | tf_op jit(solution)/shard_map/ppermute | solution.py:171
  109.8 4.9 %collective-permute-done.14.refs_15_ = bf16[8,1280,128]{2,1,0:T(8,128)(2,1)} collective-permute-done((bf16[8,1280,128]{2,1,0:T(8,128)(2,1)}, bf16[8,1280,128]{2,1,0:T(8,128)(2,1)}, u32[]{:S(2)}, u32[]{:S(2)}) %collective-permute-start.14) | collective-permute-done | bytes 2621472 | tf_op jit(solution)/shard_map/ppermute | solution.py:176
  119.4 15.9 %project.2.refs_1_.refs_16_ = f32[384,1920]{1,0:T(8,128)} custom-call(s32[5]{0:T(128)S(1)} %copy-done.20, bf16[96,5120]{1,0:T(8,128)(2,1)} %bitcast.5.refs_0_, bf16[96,5120]{1,0:T(8,128)(2,1)} %after.17.refs_2_.refs_1_, bf16[96,5120]{1,0:T(8,128)(2,1)S(1)} %copy-done.1, bf16[96,5120]{1,0:T(8,128)(2,1)} %collective-permute-done.6.refs_1_.refs_3_, ...), custom_call_target="tpu_custom_call" | custom-call | bytes 98304 | tf_op jit(solution)/shard_map/project/pallas_call | solution.py:423
  137.5 3.1 %collective-permute-done.18.refs_15_ = bf16[7,640,128]{2,1,0:T(8,128)(2,1)} collective-permute-done((bf16[7,640,128]{2,1,0:T(8,128)(2,1)}, bf16[7,640,128]{2,1,0:T(8,128)(2,1)}, u32[]{:S(2)}, u32[]{:S(2)}) %collective-permute-start.18) | collective-permute-done | bytes 1146912 | tf_op jit(solution)/shard_map/ppermute | solution.py:176
  140.5 8.6 %project.3 = (bf16[5,384,128]{2,1,0:T(8,128)(2,1)S(1)}, bf16[5,384,128]{2,1,0:T(8,128)(2,1)}, bf16[5,384,128]{2,1,0:T(8,128)(2,1)}, bf16[5,384,128]{2,1,0:T(8,128)(2,1)}, bf16[384,128]{1,0:T(8,128)(2,1)S(1)}) custom-call(s32[3]{0:T(128)S(1)} %add_add_fusion.1.order_ref, bf16[96,5120]{1,0:T(8,128)(2,1)} %bitcast.5.refs_0_, ...), custom_call_target="tpu_custom_call" | custom-call | bytes 98304 | tf_op jit(solution)/shard_map/project/pallas_call | solution.py:423
  150.1 2.6 %collective-permute-start.21 = (bf16[5,384,128]{2,1,0:T(8,128)(2,1)}, bf16[5,384,128]{2,1,0:T(8,128)(2,1)S(1)}, u32[]{:S(2)}, u32[]{:S(2)}) collective-permute-start(bf16[5,384,128]{2,1,0:T(8,128)(2,1)} %get-tuple-element.21), channel_id=1, source_target_pairs={{0,24},{8,16},{16,8},{24,0},{1,25},{9,17},{17,9},{25,1},{2,26},{10... | collective-permute-start | bytes 1474568 | tf_op jit(solution)/shard_map/ppermute | solution.py:176
  153.1 10.3 %collective-permute-done.19.refs_1_ = bf16[5,384,128]{2,1,0:T(8,128)(2,1)S(1)} collective-permute-done((bf16[5,384,128]{2,1,0:T(8,128)(2,1)}, bf16[5,384,128]{2,1,0:T(8,128)(2,1)S(1)}, u32[]{:S(2)}, u32[]{:S(2)}) %collective-permute-start.19) | collective-permute-done | bytes 491552 | tf_op jit(solution)/shard_map/ppermute | solution.py:176
  163.4 9.8 %collective-permute-done.20.refs_2_ = bf16[5,384,128]{2,1,0:T(8,128)(2,1)S(1)} collective-permute-done((bf16[5,384,128]{2,1,0:T(8,128)(2,1)}, bf16[5,384,128]{2,1,0:T(8,128)(2,1)S(1)}, u32[]{:S(2)}, u32[]{:S(2)}) %collective-permute-start.20) | collective-permute-done | bytes 491552 | tf_op jit(solution)/shard_map/ppermute | solution.py:176
  173.3 4.3 %attend.1 = (bf16[480,128]{1,0:T(8,128)(2,1)S(1)}, bf16[480,128]{1,0:T(8,128)(2,1)S(1)}, bf16[480,128]{1,0:T(8,128)(2,1)S(1)}, bf16[480,128]{1,0:T(8,128)(2,1)S(1)}) custom-call(s32[25]{0:T(128)S(1)} %pad_add_fusion.2.table_ref, bf16[5,384,128]{2,1,0:T(8,128)(2,1)S(1)} %get-tuple-element.18.refs_0_, ...), custom_call_target="tpu_custom_call" | custom-call | bytes 98304 | tf_op jit(solution)/shard_map/attend/pallas_call | solution.py:480
  181.0 3.3 %collective-permute-start.23 = (bf16[480,128]{1,0:T(8,128)(2,1)}, bf16[480,128]{1,0:T(8,128)(2,1)S(1)}, u32[]{:S(2)}, u32[]{:S(2)}) collective-permute-start(bf16[480,128]{1,0:T(8,128)(2,1)} %copy-done.21), channel_id=1, source_target_pairs={{0,4},{2,6},{4,0},{6,2},{1,5},{3,7},{5,1},{7,3},{8,12},{10,14},{12... | collective-permute-start | bytes 368648 | tf_op jit(solution)/shard_map/ppermute | solution.py:171
  184.3 3.9 %collective-permute-done.24 = bf16[480,128]{1,0:T(8,128)(2,1)S(1)} collective-permute-done((bf16[480,128]{1,0:T(8,128)(2,1)}, bf16[480,128]{1,0:T(8,128)(2,1)S(1)}, u32[]{:S(2)}, u32[]{:S(2)}) %collective-permute-start.24) | collective-permute-done | bytes 122912 | tf_op jit(solution)/shard_map/ppermute | solution.py:171
  188.2 5.0 %collective-permute-done.23 = bf16[480,128]{1,0:T(8,128)(2,1)S(1)} collective-permute-done((bf16[480,128]{1,0:T(8,128)(2,1)}, bf16[480,128]{1,0:T(8,128)(2,1)S(1)}, u32[]{:S(2)}, u32[]{:S(2)}) %collective-permute-start.23) | collective-permute-done | bytes 122912 | tf_op jit(solution)/shard_map/ppermute | solution.py:171
  197.6 10.8 %collective-permute-done.25.refs_1_ = bf16[4,480,128]{2,1,0:T(8,128)(2,1)} collective-permute-done((bf16[4,480,128]{2,1,0:T(8,128)(2,1)}, bf16[4,480,128]{2,1,0:T(8,128)(2,1)}, u32[]{:S(2)}, u32[]{:S(2)}) %collective-permute-start.25) | collective-permute-done | bytes 491552 | tf_op jit(solution)/shard_map/ppermute | solution.py:176
  208.5 11.0 %collective-permute-done.26.refs_2_ = bf16[4,480,128]{2,1,0:T(8,128)(2,1)} collective-permute-done((bf16[4,480,128]{2,1,0:T(8,128)(2,1)}, bf16[4,480,128]{2,1,0:T(8,128)(2,1)}, u32[]{:S(2)}, u32[]{:S(2)}) %collective-permute-start.26) | collective-permute-done | bytes 491552 | tf_op jit(solution)/shard_map/ppermute | solution.py:176
  221.4 7.9 %out_project.1 = (bf16[96,1280]{1,0:T(8,128)(2,1)S(1)}, bf16[96,1280]{1,0:T(8,128)(2,1)S(1)}, bf16[96,1280]{1,0:T(8,128)(2,1)S(1)}, bf16[96,1280]{1,0:T(8,128)(2,1)S(1)}) custom-call(s32[3]{0:T(128)S(1)} %add_add_fusion.at_ref, bf16[4,480,128]{2,1,0:T(8,128)(2,1)} %pad_maximum_fusion.1.refs_0_, bf16[4,480,128]{2,1,0:T(8,128)(2,1)} %collective-permute-done.25.refs_1_, ...), custom_call_target="tpu_custom_call" | custom-call | bytes 983040 | tf_op jit(solution)/shard_map/out_project/pallas_call | solution.py:540
  233.5 5.4 %collective-permute-done.29.refs_1_ = bf16[96,1280]{1,0:T(8,128)(2,1)S(1)} collective-permute-done((bf16[96,1280]{1,0:T(8,128)(2,1)S(1)}, bf16[96,1280]{1,0:T(8,128)(2,1)S(1)}, u32[]{:S(2)}, u32[]{:S(2)}) %collective-permute-start.29) | collective-permute-done | bytes 245792 | tf_op jit(solution)/shard_map/ppermute | solution.py:176
  238.9 3.4 %collective-permute-done.30.refs_2_ = bf16[96,1280]{1,0:T(8,128)(2,1)S(1)} collective-permute-done((bf16[96,1280]{1,0:T(8,128)(2,1)S(1)}, bf16[96,1280]{1,0:T(8,128)(2,1)S(1)}, u32[]{:S(2)}, u32[]{:S(2)}) %collective-permute-start.30) | collective-permute-done | bytes 245792 | tf_op jit(solution)/shard_map/ppermute | solution.py:176
  243.1 2.3 place_columns.1
  (164 shorter events, 50.1 us)
Async XLA Ops:
  6.5 173.0 %all-gather.3.cloned.1.call-start = ((), (), s32[]{:S(2)}) async-start(), calls=%async_computation | async-start | bytes 4096000 | tf_op jit(solution)/shard_map/all_gather | solution.py:656
  9.9 37.3 %collective-permute-start.8 = (bf16[8,1280,128]{2,1,0:T(8,128)(2,1)}, bf16[8,1280,128]{2,1,0:T(8,128)(2,1)S(1)}, u32[]{:S(2)}, u32[]{:S(2)}) collective-permute-start(bf16[8,1280,128]{2,1,0:T(8,128)(2,1)} %slice.19), channel_id=1, source_target_pairs={{0,8},{1,17},{8,0},{9,25},{16,24},{17,1},{24,16},{25,9},{2,10},{3,... | collective-permute-start | bytes 7864328 | tf_op jit(solution)/shard_map/ppermute | solution.py:598
  12.9 33.7 %collective-permute-start = (bf16[96,5120]{1,0:T(8,128)(2,1)}, bf16[96,5120]{1,0:T(8,128)(2,1)}, u32[]{:S(2)}, u32[]{:S(2)}) collective-permute-start(bf16[96,5120]{1,0:T(8,128)(2,1)} %bitcast.5.refs_0_), channel_id=1, source_target_pairs={{0,2},{2,4},{4,6},{1,3},{3,5},{5,7},{8,10},{10,12},{12,14},{9,11},... | collective-permute-start | bytes 2949128 | tf_op jit(solution)/shard_map/ppermute | solution.py:181
  17.4 29.8 %collective-permute-start.4 = (bf16[96,5120]{1,0:T(8,128)(2,1)}, bf16[96,5120]{1,0:T(8,128)(2,1)}, u32[]{:S(2)}, u32[]{:S(2)}) collective-permute-start(bf16[96,5120]{1,0:T(8,128)(2,1)} %bitcast.5.refs_0_), channel_id=1, source_target_pairs={{2,0},{4,2},{6,4},{3,1},{5,3},{7,5},{10,8},{12,10},{14,12},{11,9},... | collective-permute-start | bytes 2949128 | tf_op jit(solution)/shard_map/ppermute | solution.py:182
  22.7 23.9 %collective-permute-start.1 = (bf16[2,4,48,256]{3,2,1,0:T(8,128)(2,1)}, bf16[2,4,48,256]{3,2,1,0:T(8,128)(2,1)S(1)}, u32[]{:S(2)}, u32[]{:S(2)}) collective-permute-start(bf16[2,4,48,256]{3,2,1,0:T(8,128)(2,1)} %after.16), channel_id=1, source_target_pairs={{0,8},{8,16},{16,24},{1,9},{9,17},{17,25},{2,10},{10,18},{18,26},{... | collective-permute-start | bytes 589832 | tf_op jit(solution)/shard_map/ppermute | solution.py:23
  48.8 40.9 %collective-permute-start.9 = (bf16[7,1280,128]{2,1,0:T(8,128)(2,1)}, bf16[7,1280,128]{2,1,0:T(8,128)(2,1)S(1)}, u32[]{:S(2)}, u32[]{:S(2)}) collective-permute-start(bf16[7,1280,128]{2,1,0:T(8,128)(2,1)} %after.22), channel_id=1, source_target_pairs={{0,8},{1,17},{8,0},{9,25},{16,24},{17,1},{24,16},{25,9},{2,10},{3,... | collective-permute-start | bytes 6881288 | tf_op jit(solution)/shard_map/ppermute | solution.py:607
  51.2 12.5 %collective-permute-start.2 = (bf16[96,5120]{1,0:T(8,128)(2,1)}, bf16[96,5120]{1,0:T(8,128)(2,1)S(1)}, u32[]{:S(2)}, u32[]{:S(2)}) collective-permute-start(bf16[96,5120]{1,0:T(8,128)(2,1)} %after.17.refs_2_.refs_1_), channel_id=1, source_target_pairs={{2,4},{4,6},{3,5},{5,7},{10,12},{12,14},{11,13},{13,15},{18,20},{2... | collective-permute-start | bytes 2949128 | tf_op jit(solution)/shard_map/ppermute | solution.py:181
  51.9 23.9 %collective-permute-start.5 = (bf16[96,5120]{1,0:T(8,128)(2,1)}, bf16[96,5120]{1,0:T(8,128)(2,1)}, u32[]{:S(2)}, u32[]{:S(2)}) collective-permute-start(bf16[96,5120]{1,0:T(8,128)(2,1)} %after.19.refs_3_.refs_4_), channel_id=1, source_target_pairs={{2,0},{4,2},{3,1},{5,3},{10,8},{12,10},{11,9},{13,11},{18,16},{20,... | collective-permute-start | bytes 2949128 | tf_op jit(solution)/shard_map/ppermute | solution.py:182
  54.5 9.1 %collective-permute-start.3 = (bf16[4,1,48,256]{3,2,1,0:T(8,128)(2,1)S(1)}, bf16[4,1,48,256]{3,2,1,0:T(8,128)(2,1)S(1)}, u32[]{:S(2)}, u32[]{:S(2)}) collective-permute-start(bf16[4,1,48,256]{3,2,1,0:T(8,128)(2,1)S(1)} %slice.17), channel_id=1, source_target_pairs={{0,2},{2,4},{4,6},{1,3},{3,5},{5,7},{8,10},{10,12},{12,14},{9,11},... | collective-permute-start | bytes 294920 | tf_op jit(solution)/shard_map/ppermute | solution.py:23
  65.2 39.0 %collective-permute-start.6 = (bf16[96,5120]{1,0:T(8,128)(2,1)}, bf16[96,5120]{1,0:T(8,128)(2,1)}, u32[]{:S(2)}, u32[]{:S(2)}) collective-permute-start(bf16[96,5120]{1,0:T(8,128)(2,1)} %after.18.refs_1_.refs_2_), channel_id=1, source_target_pairs={{4,6},{5,7},{12,14},{13,15},{20,22},{21,23},{28,30},{29,31}} | collective-permute-start | bytes 2949128 | tf_op jit(solution)/shard_map/ppermute | solution.py:181
  75.8 28.4 %collective-permute-start.7 = (bf16[96,5120]{1,0:T(8,128)(2,1)}, bf16[96,5120]{1,0:T(8,128)(2,1)}, u32[]{:S(2)}, u32[]{:S(2)}) collective-permute-start(bf16[96,5120]{1,0:T(8,128)(2,1)} %after.20.refs_2_.refs_5_), channel_id=1, source_target_pairs={{2,0},{3,1},{10,8},{11,9},{18,16},{19,17},{26,24},{27,25}} | collective-permute-start | bytes 2949128 | tf_op jit(solution)/shard_map/ppermute | solution.py:182
  93.5 10.8 %collective-permute-start.10 = (bf16[96,320]{1,0:T(8,128)(2,1)}, bf16[96,320]{1,0:T(8,128)(2,1)S(1)}, u32[]{:S(2)}, u32[]{:S(2)}) collective-permute-start(bf16[96,320]{1,0:T(8,128)(2,1)} %after.25.refs_7_), channel_id=1, source_target_pairs={{0,2},{2,4},{4,6},{6,0},{1,3},{3,5},{5,7},{7,1},{8,10},{10,12},{12... | collective-permute-start | bytes 184328 | tf_op jit(solution)/shard_map/ppermute | solution.py:171
  97.2 7.1 %collective-permute-start.11 = (bf16[96,320]{1,0:T(8,128)(2,1)}, bf16[96,320]{1,0:T(8,128)(2,1)S(1)}, u32[]{:S(2)}, u32[]{:S(2)}) collective-permute-start(bf16[96,320]{1,0:T(8,128)(2,1)} %after.25.refs_7_), channel_id=1, source_target_pairs={{0,4},{2,6},{4,0},{6,2},{1,5},{3,7},{5,1},{7,3},{8,12},{10,14},{12... | collective-permute-start | bytes 184328 | tf_op jit(solution)/shard_map/ppermute | solution.py:171
  101.4 5.1 %collective-permute-start.12 = (bf16[96,320]{1,0:T(8,128)(2,1)}, bf16[96,320]{1,0:T(8,128)(2,1)}, u32[]{:S(2)}, u32[]{:S(2)}) collective-permute-start(bf16[96,320]{1,0:T(8,128)(2,1)} %after.25.refs_7_), channel_id=1, source_target_pairs={{0,6},{2,0},{4,2},{6,4},{1,7},{3,1},{5,3},{7,5},{8,14},{10,8},{12,... | collective-permute-start | bytes 184328 | tf_op jit(solution)/shard_map/ppermute | solution.py:171
  106.6 8.2 %collective-permute-start.14 = (bf16[8,1280,128]{2,1,0:T(8,128)(2,1)}, bf16[8,1280,128]{2,1,0:T(8,128)(2,1)}, u32[]{:S(2)}, u32[]{:S(2)}) collective-permute-start(bf16[8,1280,128]{2,1,0:T(8,128)(2,1)} %copy-done.4), channel_id=1, source_target_pairs={{0,1},{1,0},{2,3},{3,2},{4,5},{5,4},{6,7},{7,6},{8,9},{9,8},{10,11... | collective-permute-start | bytes 7864328 | tf_op jit(solution)/shard_map/ppermute | solution.py:176
  106.7 8.3 %collective-permute-start.15 = (bf16[7,1280,128]{2,1,0:T(8,128)(2,1)S(1)}, bf16[7,1280,128]{2,1,0:T(8,128)(2,1)}, u32[]{:S(2)}, u32[]{:S(2)}) collective-permute-start(bf16[7,1280,128]{2,1,0:T(8,128)(2,1)S(1)} %copy-done.3), channel_id=1, source_target_pairs={{0,1},{1,0},{2,3},{3,2},{4,5},{5,4},{6,7},{7,6},{8,9},{9,8},{10,11... | collective-permute-start | bytes 6881288 | tf_op jit(solution)/shard_map/ppermute | solution.py:176
  107.2 28.1 %collective-permute-start.13 = (bf16[8,640,128]{2,1,0:T(8,128)(2,1)}, bf16[8,640,128]{2,1,0:T(8,128)(2,1)}, u32[]{:S(2)}, u32[]{:S(2)}) collective-permute-start(bf16[8,640,128]{2,1,0:T(8,128)(2,1)} %after.23.refs_3_), channel_id=1, source_target_pairs={{0,16},{1,9},{8,24},{9,1},{16,0},{17,25},{24,8},{25,17},{2,18},{3,... | collective-permute-start | bytes 3932168 | tf_op jit(solution)/shard_map/ppermute | solution.py:631
  107.6 29.7 %collective-permute-start.16 = (bf16[7,640,128]{2,1,0:T(8,128)(2,1)}, bf16[7,640,128]{2,1,0:T(8,128)(2,1)}, u32[]{:S(2)}, u32[]{:S(2)}) collective-permute-start(bf16[7,640,128]{2,1,0:T(8,128)(2,1)} %after.29), channel_id=1, source_target_pairs={{0,16},{1,9},{8,24},{9,1},{16,0},{17,25},{24,8},{25,17},{2,18},{3,... | collective-permute-start | bytes 3440648 | tf_op jit(solution)/shard_map/ppermute | solution.py:631
  135.3 5.2 %collective-permute-start.17 = (bf16[8,640,128]{2,1,0:T(8,128)(2,1)}, bf16[8,640,128]{2,1,0:T(8,128)(2,1)S(1)}, u32[]{:S(2)}, u32[]{:S(2)}) collective-permute-start(bf16[8,640,128]{2,1,0:T(8,128)(2,1)} %after.28.refs_12_), channel_id=1, source_target_pairs={{0,1},{1,0},{2,3},{3,2},{4,5},{5,4},{6,7},{7,6},{8,9},{9,8},{10,11... | collective-permute-start | bytes 3932168 | tf_op jit(solution)/shard_map/ppermute | solution.py:176
  149.1 14.3 %collective-permute-start.19 = (bf16[5,384,128]{2,1,0:T(8,128)(2,1)}, bf16[5,384,128]{2,1,0:T(8,128)(2,1)S(1)}, u32[]{:S(2)}, u32[]{:S(2)}) collective-permute-start(bf16[5,384,128]{2,1,0:T(8,128)(2,1)} %get-tuple-element.19), channel_id=1, source_target_pairs={{0,8},{8,0},{16,24},{24,16},{1,9},{9,1},{17,25},{25,17},{2,10},{10... | collective-permute-start | bytes 1474568 | tf_op jit(solution)/shard_map/ppermute | solution.py:176
  149.2 24.1 %collective-permute-start.20 = (bf16[5,384,128]{2,1,0:T(8,128)(2,1)}, bf16[5,384,128]{2,1,0:T(8,128)(2,1)S(1)}, u32[]{:S(2)}, u32[]{:S(2)}) collective-permute-start(bf16[5,384,128]{2,1,0:T(8,128)(2,1)} %get-tuple-element.20), channel_id=1, source_target_pairs={{0,16},{8,24},{16,0},{24,8},{1,17},{9,25},{17,1},{25,9},{2,18},{10... | collective-permute-start | bytes 1474568 | tf_op jit(solution)/shard_map/ppermute | solution.py:176
  150.1 23.2 %collective-permute-start.21 = (bf16[5,384,128]{2,1,0:T(8,128)(2,1)}, bf16[5,384,128]{2,1,0:T(8,128)(2,1)S(1)}, u32[]{:S(2)}, u32[]{:S(2)}) collective-permute-start(bf16[5,384,128]{2,1,0:T(8,128)(2,1)} %get-tuple-element.21), channel_id=1, source_target_pairs={{0,24},{8,16},{16,8},{24,0},{1,25},{9,17},{17,9},{25,1},{2,26},{10... | collective-permute-start | bytes 1474568 | tf_op jit(solution)/shard_map/ppermute | solution.py:176
  179.6 39.9 %collective-permute-start.28 = (bf16[4,640,640]{2,1,0:T(8,128)(2,1)}, bf16[4,640,640]{2,1,0:T(8,128)(2,1)S(1)}, u32[]{:S(2)}, u32[]{:S(2)}) collective-permute-start(bf16[4,640,640]{2,1,0:T(8,128)(2,1)} %after.31.refs_4_), channel_id=1, source_target_pairs={{0,1},{1,0},{2,3},{3,2},{4,5},{5,4},{6,7},{7,6},{8,9},{9,8},{10,11... | collective-permute-start | bytes 9830408 | tf_op jit(solution)/shard_map/ppermute | solution.py:176
  179.6 8.7 %collective-permute-start.24 = (bf16[480,128]{1,0:T(8,128)(2,1)}, bf16[480,128]{1,0:T(8,128)(2,1)S(1)}, u32[]{:S(2)}, u32[]{:S(2)}) collective-permute-start(bf16[480,128]{1,0:T(8,128)(2,1)} %copy-done.22), channel_id=1, source_target_pairs={{0,2},{2,4},{4,6},{6,0},{1,3},{3,5},{5,7},{7,1},{8,10},{10,12},{12... | collective-permute-start | bytes 368648 | tf_op jit(solution)/shard_map/ppermute | solution.py:171
  181.0 12.2 %collective-permute-start.23 = (bf16[480,128]{1,0:T(8,128)(2,1)}, bf16[480,128]{1,0:T(8,128)(2,1)S(1)}, u32[]{:S(2)}, u32[]{:S(2)}) collective-permute-start(bf16[480,128]{1,0:T(8,128)(2,1)} %copy-done.21), channel_id=1, source_target_pairs={{0,4},{2,6},{4,0},{6,2},{1,5},{3,7},{5,1},{7,3},{8,12},{10,14},{12... | collective-permute-start | bytes 368648 | tf_op jit(solution)/shard_map/ppermute | solution.py:171
  184.3 8.9 %collective-permute-start.22 = (bf16[480,128]{1,0:T(8,128)(2,1)S(1)}, bf16[480,128]{1,0:T(8,128)(2,1)S(1)}, u32[]{:S(2)}, u32[]{:S(2)}) collective-permute-start(bf16[480,128]{1,0:T(8,128)(2,1)S(1)} %get-tuple-element.24), channel_id=1, source_target_pairs={{0,6},{2,0},{4,2},{6,4},{1,7},{3,1},{5,3},{7,5},{8,14},{10,8},{12,... | collective-permute-start | bytes 368648 | tf_op jit(solution)/shard_map/ppermute | solution.py:171
  194.1 14.4 %collective-permute-start.25 = (bf16[4,480,128]{2,1,0:T(8,128)(2,1)}, bf16[4,480,128]{2,1,0:T(8,128)(2,1)}, u32[]{:S(2)}, u32[]{:S(2)}) collective-permute-start(bf16[4,480,128]{2,1,0:T(8,128)(2,1)} %pad_maximum_fusion.1.refs_0_), channel_id=1, source_target_pairs={{0,8},{8,0},{16,24},{24,16},{1,9},{9,1},{17,25},{25,17},{2,10},{10... | collective-permute-start | bytes 1474568 | tf_op jit(solution)/shard_map/ppermute | solution.py:176
  195.7 23.7 %collective-permute-start.26 = (bf16[4,480,128]{2,1,0:T(8,128)(2,1)}, bf16[4,480,128]{2,1,0:T(8,128)(2,1)}, u32[]{:S(2)}, u32[]{:S(2)}) collective-permute-start(bf16[4,480,128]{2,1,0:T(8,128)(2,1)} %pad_maximum_fusion.1.refs_0_), channel_id=1, source_target_pairs={{0,16},{8,24},{16,0},{24,8},{1,17},{9,25},{17,1},{25,9},{2,18},{10... | collective-permute-start | bytes 1474568 | tf_op jit(solution)/shard_map/ppermute | solution.py:176
  196.2 23.2 %collective-permute-start.27 = (bf16[4,480,128]{2,1,0:T(8,128)(2,1)}, bf16[4,480,128]{2,1,0:T(8,128)(2,1)}, u32[]{:S(2)}, u32[]{:S(2)}) collective-permute-start(bf16[4,480,128]{2,1,0:T(8,128)(2,1)} %pad_maximum_fusion.1.refs_0_), channel_id=1, source_target_pairs={{0,24},{8,16},{16,8},{24,0},{1,25},{9,17},{17,9},{25,1},{2,26},{10... | collective-permute-start | bytes 1474568 | tf_op jit(solution)/shard_map/ppermute | solution.py:176
  230.0 8.9 %collective-permute-start.29 = (bf16[96,1280]{1,0:T(8,128)(2,1)S(1)}, bf16[96,1280]{1,0:T(8,128)(2,1)S(1)}, u32[]{:S(2)}, u32[]{:S(2)}) collective-permute-start(bf16[96,1280]{1,0:T(8,128)(2,1)S(1)} %get-tuple-element.28), channel_id=1, source_target_pairs={{0,8},{8,0},{16,24},{24,16},{1,9},{9,1},{17,25},{25,17},{2,10},{10... | collective-permute-start | bytes 737288 | tf_op jit(solution)/shard_map/ppermute | solution.py:176
  230.4 11.9 %collective-permute-start.30 = (bf16[96,1280]{1,0:T(8,128)(2,1)S(1)}, bf16[96,1280]{1,0:T(8,128)(2,1)S(1)}, u32[]{:S(2)}, u32[]{:S(2)}) collective-permute-start(bf16[96,1280]{1,0:T(8,128)(2,1)S(1)} %get-tuple-element.29), channel_id=1, source_target_pairs={{0,16},{8,24},{16,0},{24,8},{1,17},{9,25},{17,1},{25,9},{2,18},{10... | collective-permute-start | bytes 737288 | tf_op jit(solution)/shard_map/ppermute | solution.py:176
  231.8 10.5 %collective-permute-start.31 = (bf16[96,1280]{1,0:T(8,128)(2,1)S(1)}, bf16[96,1280]{1,0:T(8,128)(2,1)S(1)}, u32[]{:S(2)}, u32[]{:S(2)}) collective-permute-start(bf16[96,1280]{1,0:T(8,128)(2,1)S(1)} %get-tuple-element.30), channel_id=1, source_target_pairs={{0,24},{8,16},{16,8},{24,0},{1,25},{9,17},{17,9},{25,1},{2,26},{10... | collective-permute-start | bytes 737288 | tf_op jit(solution)/shard_map/ppermute | solution.py:176
  (38 other events, 204.0 us)
Sparse Core Ops, SparseCore 0:
  106.7 65.5 all-gather.2
where the time goes:
time: 253 us; the launch traced here: 252 us
  waiting for transfers between devices  105 us (42%)
  starting transfers between devices  54.3 us (21%)
  Pallas kernels  45.4 us (18%)
  local copies, waits for them, and re-layouts  31.3 us (12%)
  between operations  13.8 us (5%)
  other arithmetic  2.85 us (1%)
    ppermute x14, waiting for transfers between devices, across(): return lax.ppermute(value, axis, [(i, i ^ bits) for i in range(count)])  59 us
    pallas_call x2, Pallas kernels, project(): pl.pallas_call(body, out_shape=out_shape, grid_spec=pltpu.PrefetchScalarG...  24.5 us
    ppermute x2, waiting for transfers between devices, shifted(): lax.ppermute(value, axis, [(source, source + steps) for source in range(l...  23.6 us
    unnamed x76, local copies, waits for them, and re-layouts  18.5 us
    ppermute x6, starting transfers between devices, turn(): lax.ppermute(value, axis, [(i, (i + steps) % count) for i in range(count)])  15.5 us
    ppermute x14, starting transfers between devices, across(): return lax.ppermute(value, axis, [(i, i ^ bits) for i in range(count)])  11.3 us
    ppermute x6, waiting for transfers between devices, turn(): lax.ppermute(value, axis, [(i, (i + steps) % count) for i in range(count)])  11.2 us
    ppermute x2, starting transfers between devices, shifted(): lax.ppermute(value, axis, [(source, source + steps) for source in range(l...  9.37 us
  transfers between devices with their start and end apart: 33, of which 16 were waited for; matrix products, arithmetic and copies ran while one was open for 5% of the time, Pallas kernels for 14%

commit v1 on v0

--- a/solution.py
+++ b/solution.py
@@ -499,16 +499,19 @@
     heads = depth // size
 
     def body(at_ref, *refs):
-        weight_refs = refs[PLANE : PLANE + 2]
-        out_refs, lhs_ref, sum_ref = refs[PLANE + 2 : -2], refs[-2], refs[-1]
+        weight_refs = refs[PLANE + 1 : PLANE + 3]
+        out_refs, lhs_ref, sum_ref = refs[PLANE + 3 : -2], refs[-2], refs[-1]
         step = pl.program_id(0)
-        for p in range(PLANE):
-            rows = slice(p * tokens, (p + 1) * tokens)
-            for q in range(PLANE):
+        def put(q, ref):
+            for p in range(PLANE):
                 at = (p ^ q) * tokens
-                lhs_ref[rows, q * size : (q + 1) * size] = refs[q][0, at : at + tokens]
-            lhs_ref[rows, PLANE * size :] = refs[p][0, PLANE * tokens :]
-
+                lhs_ref[p * tokens : (p + 1) * tokens, q * size : (q + 1) * size] = ref[0, at : at + tokens]
+            lhs_ref[q * tokens : (q + 1) * tokens, PLANE * size :] = ref[0, PLANE * tokens :]
+
+        for q in range(PLANE - 1):
+            put(q, refs[q])
+        pl.when(step < groups // 2)(lambda: put(PLANE - 1, refs[PLANE - 1]))
+        pl.when(step >= groups // 2)(lambda: put(PLANE - 1, refs[PLANE]))
         here_at, core_at = at_ref[0], at_ref[2]
         for c in range(2):
             found = [
@@ -533,7 +536,12 @@
                     at = pl.multiple_of((core_at ^ c) * columns, 128)
                     out_refs[p][:, pl.ds(at, columns)] = sum_ref[c, p * tokens : (p + 1) * tokens].astype(BF16)
 
-    in_specs = [pl.BlockSpec((1,) + piece.shape[1:], lambda g, at: (g, 0, 0)) for piece in gathered]
+    block = (1,) + gathered[0].shape[1:]
+    in_specs = [pl.BlockSpec(block, lambda g, at: (g, 0, 0))] * (PLANE - 1)
+    in_specs += [
+        pl.BlockSpec(block, lambda g, at: (jnp.minimum(g, groups // 2 - 1), 0, 0)),
+        pl.BlockSpec(block, lambda g, at: (jnp.maximum(g - groups // 2, 0), 0, 0)),
+    ]
     in_specs += [
         pl.BlockSpec((1, depth, columns), lambda g, at: (lax.rem(at[1] + g, groups), 0, 0))
     ] * 2
@@ -602,8 +610,7 @@
     own = latent.reshape(tokens, model_width)
     lower, upper = hop(own, own, "head", 1)
     lower, upper = [lower], [upper]
-    lower[0], upper[0] = after(lower[0], earlier), after(upper[0], earlier)
-    near_rest = after(near_rest, near_first, lower[0], upper[0])
+    near_rest = after(near_rest, near_first, earlier, lower[0], upper[0])
     near_rest = lax.ppermute(near_rest, plane_axes, near_pairs)
     extended = jnp.concatenate([earlier, pose_maps], axis=0)
     rows_above = shifted(extended[:, -1:], "head", 1)
@@ -619,17 +626,14 @@
             below, above = after(below, rows_above), after(above, rows_above)
         lower.append(below)
         upper.append(above)
-    start_of = after(start_of, lower[1], upper[1], out_half)
-    feature = pose_feature(extended, conv_weight, conv_bias, start_of, here * frames)
     half_rows = weight.shape[1] // 2
     first_half = lax.dynamic_slice_in_dim(near_first, core * half_rows, half_rows, axis=1)
-    first_half = after(first_half, lower[1])
-    near_rest = after(near_rest, lower[1], upper[1], first_half)
+    near_rest = after(near_rest, lower[1], upper[1], first_half, out_half)
     near = (near_first, near_rest)
     rest_half = lax.dynamic_slice_in_dim(near_rest, core * half_rows, half_rows, axis=1)
-    rest_half = after(rest_half, feature)
     far = tuple(lax.ppermute(part, plane_axes, far_pairs) for part in (first_half, rest_half))
-    feature = after(feature, near_rest)
+    start_of = after(start_of, rest_half)
+    feature = pose_feature(extended, conv_weight, conv_bias, start_of, here * frames)
     features = [feature] + [turn(feature, "head", s) for s in range(1, strips)]
     other = tuple(across(part, "dp", 1) for part in near)
     out_half = after(out_half, lower[-1], upper[-1], *features[1:])
@@ -657,8 +661,11 @@
     out_weights = [out_half, across(out_half, "dp", 1)]
 
     strip_heads = [outs[0]] + [turn(outs[s], "head", -s) for s in range(1, strips)]
-    strip_heads = jnp.stack(strip_heads)
-    gathered = [strip_heads] + [across(strip_heads, "frame", r) for r in range(1, PLANE)]
+    strip_heads = after(jnp.stack(strip_heads), out_weights[1])
+    from_x, from_y = across(strip_heads, "frame", 1), across(strip_heads, "frame", 2)
+    middle = strips // 2
+    gathered = [strip_heads, from_x, from_y]
+    gathered += [across(from_y[:middle], "frame", 1), across(from_x[middle:], "frame", 2)]
     done = out_project(gathered, out_weights, here, group, core, tokens)
     mine = [done[0]] + [across(done[r], "frame", r) for r in range(1, PLANE)]
     return place_columns(mine, here).reshape(latent.shape)

time: 253 us -> 261 us (1.032)
  local copies, waits for them, and re-layouts: 31.3 us -> 41.3 us
  waiting for transfers between devices: 105 us -> 98.5 us
    unnamed x76 -> x90, local copies, waits for them, and re-layouts: 18.5 us -> 26.9 us
    ppermute x14 -> x15, waiting for transfers between devices: 59 us -> 55.2 us  [across(): return lax.ppermute(value, axis, [(i, i ^ bits) for i in range(count)])]
    ppermute x14 -> x15, starting transfers between devices: 11.3 us -> 12.2 us  [across(): return lax.ppermute(value, axis, [(i, i ^ bits) for i in range(count)])]
  transfers between devices with their start and end apart: 33 -> 34, of which waited for: 16 -> 17; matrix products, arithmetic and copies ran while one was open for 5% -> 7% of each run, Pallas kernels for 14% -> 13%
where the time goes in v1:
time: 261 us; the launch traced here: 259 us
  waiting for transfers between devices  98.5 us (38%)
  starting transfers between devices  55.6 us (21%)
  Pallas kernels  45.5 us (17%)
  local copies, waits for them, and re-layouts  41.3 us (16%)
  between operations  13.8 us (5%)
  other arithmetic  4.76 us (2%)
    ppermute x15, waiting for transfers between devices, across(): return lax.ppermute(value, axis, [(i, i ^ bits) for i in range(count)])  55.2 us
    unnamed x90, local copies, waits for them, and re-layouts  26.9 us
    pallas_call x2, Pallas kernels, project(): pl.pallas_call(body, out_shape=out_shape, grid_spec=pltpu.PrefetchScalarG...  24.1 us
    ppermute x2, waiting for transfers between devices, shifted(): lax.ppermute(value, axis, [(source, source + steps) for source in range(l...  23.5 us
    ppermute x6, starting transfers between devices, turn(): lax.ppermute(value, axis, [(i, (i + steps) % count) for i in range(count)])  15.7 us
    ppermute x15, starting transfers between devices, across(): return lax.ppermute(value, axis, [(i, i ^ bits) for i in range(count)])  12.2 us
    ppermute x6, waiting for transfers between devices, turn(): lax.ppermute(value, axis, [(i, (i + steps) % count) for i in range(count)])  10.6 us
    ppermute x2, starting transfers between devices, shifted(): lax.ppermute(value, axis, [(source, source + steps) for source in range(l...  9.5 us
  transfers between devices with their start and end apart: 34, of which 17 were waited for; matrix products, arithmetic and copies ran while one was open for 7% of the time, Pallas kernels for 13%

profile of v1, /device:TPU:0, one launch (start us, length us, event | category | flops | bytes accessed | tf_op | source)
XLA Modules:
  0.0 259.4 jit_solution(14218349779846096645)
XLA Ops:
  6.5 3.4 %slice.25 = bf16[8,1280,128]{2,1,0:T(8,128)(2,1)} slice(bf16[15,1280,128]{2,1,0:T(8,128)(2,1)} %bitcast.41), slice={[0:8], [0:1280], [0:128]} | slice | bytes 5242880 | tf_op jit(solution)/shard_map/slice | solution.py:606
  9.9 2.9 %collective-permute-start = (bf16[8,1280,128]{2,1,0:T(8,128)(2,1)}, bf16[8,1280,128]{2,1,0:T(8,128)(2,1)S(1)}, u32[]{:S(2)}, u32[]{:S(2)}) collective-permute-start(bf16[8,1280,128]{2,1,0:T(8,128)(2,1)} %slice.25), channel_id=1, source_target_pairs={{0,8},{1,17},{8,0},{9,25},{16,24},{17,1},{24,16},{25,9},{2,10},{3,... | collective-permute-start | bytes 7864328 | tf_op jit(solution)/shard_map/ppermute | solution.py:606
  12.9 4.6 %collective-permute-start.2 = (bf16[96,5120]{1,0:T(8,128)(2,1)}, bf16[96,5120]{1,0:T(8,128)(2,1)}, u32[]{:S(2)}, u32[]{:S(2)}) collective-permute-start(bf16[96,5120]{1,0:T(8,128)(2,1)} %bitcast.8.refs_0_), channel_id=1, source_target_pairs={{0,2},{2,4},{4,6},{1,3},{3,5},{5,7},{8,10},{10,12},{12,14},{9,11},... | collective-permute-start | bytes 2949128 | tf_op jit(solution)/shard_map/ppermute | solution.py:181
  18.7 3.2 %slice.24.refs_1_.refs_0_ = bf16[7,1280,128]{2,1,0:T(8,128)(2,1)} slice(bf16[15,1280,128]{2,1,0:T(8,128)(2,1)} %bitcast.42), slice={[8:15], [0:1280], [0:128]} | slice | bytes 4587520 | tf_op jit(solution)/shard_map/slice | solution.py:607
  22.6 2.6 collective-permute-start.1
  25.2 21.4 %collective-permute-done.1.refs_2_ = bf16[2,4,48,256]{3,2,1,0:T(8,128)(2,1)S(1)} collective-permute-done((bf16[2,4,48,256]{3,2,1,0:T(8,128)(2,1)}, bf16[2,4,48,256]{3,2,1,0:T(8,128)(2,1)S(1)}, u32[]{:S(2)}, u32[]{:S(2)}) %collective-permute-start.1) | collective-permute-done | bytes 196640 | tf_op jit(solution)/shard_map/ppermute | solution.py:23
  48.7 2.4 collective-permute-start.4
  54.4 6.9 %collective-permute-start.6 = (bf16[4,1,48,256]{3,2,1,0:T(8,128)(2,1)S(1)}, bf16[4,1,48,256]{3,2,1,0:T(8,128)(2,1)S(1)}, u32[]{:S(2)}, u32[]{:S(2)}) collective-permute-start(bf16[4,1,48,256]{3,2,1,0:T(8,128)(2,1)S(1)} %slice.26), channel_id=1, source_target_pairs={{0,2},{2,4},{4,6},{1,3},{3,5},{5,7},{8,10},{10,12},{12,14},{9,11},... | collective-permute-start | bytes 294920 | tf_op jit(solution)/shard_map/ppermute | solution.py:23
  66.8 8.8 %collective-permute-done.7.refs_0_ = bf16[96,5120]{1,0:T(8,128)(2,1)S(1)} collective-permute-done((bf16[96,5120]{1,0:T(8,128)(2,1)}, bf16[96,5120]{1,0:T(8,128)(2,1)S(1)}, u32[]{:S(2)}, u32[]{:S(2)}) %collective-permute-start.7) | collective-permute-done | bytes 983072 | tf_op jit(solution)/shard_map/ppermute | solution.py:182
  78.5 2.9 %take_block.1.refs_4_.refs_0_ = bf16[640,640]{1,0:T(8,128)(2,1)} custom-call(s32[2]{0:T(128)} %pad_add_fusion.1.at_ref, bf16[640,5120]{1,0:T(8,128)(2,1)} %bitcast.44), custom_call_target="tpu_custom_call" | custom-call | bytes 1638400 | tf_op jit(solution)/shard_map/take_block/pallas_call | solution.py:205
  87.2 2.4 constant_dynamic-slice_fusion.refs_1_
  92.6 3.4 %pose_conv.1 = bf16[2,2,24,320]{3,2,1,0:T(8,128)(2,1)S(1)} custom-call(s32[6]{0:T(128)S(1)} %reshape.86.keep_ref, bf16[4,5,24,768]{3,2,1,0:T(8,128)(2,1)S(1)} %fusion.1.cols_ref, bf16[9,3,320,256]{3,2,1,0:T(8,128)(2,1)S(1)} %bitcast.34, f32[1,320]{1,0:T(1,128)S(1)} %reshape.83.bias_ref), custom_call_target="tpu_custom_call" | custom-call | flops 30720 | bytes 61440 | tf_op jit(solution)/shard_map/pose_conv/pallas_call | solution.py:274
  96.0 3.9 %collective-permute-start.10 = (bf16[96,320]{1,0:T(8,128)(2,1)S(1)}, bf16[96,320]{1,0:T(8,128)(2,1)S(1)}, u32[]{:S(2)}, u32[]{:S(2)}) collective-permute-start(bf16[96,320]{1,0:T(8,128)(2,1)S(1)} %bitcast.35), channel_id=1, source_target_pairs={{0,2},{2,4},{4,6},{6,0},{1,3},{3,5},{5,7},{7,1},{8,10},{10,12},{12... | collective-permute-start | bytes 184328 | tf_op jit(solution)/shard_map/ppermute | solution.py:171
  99.9 4.2 %collective-permute-start.11 = (bf16[96,320]{1,0:T(8,128)(2,1)S(1)}, bf16[96,320]{1,0:T(8,128)(2,1)S(1)}, u32[]{:S(2)}, u32[]{:S(2)}) collective-permute-start(bf16[96,320]{1,0:T(8,128)(2,1)S(1)} %bitcast.36), channel_id=1, source_target_pairs={{0,4},{2,6},{4,0},{6,2},{1,5},{3,7},{5,1},{7,3},{8,12},{10,14},{12... | collective-permute-start | bytes 184328 | tf_op jit(solution)/shard_map/ppermute | solution.py:171
  104.1 2.8 %collective-permute-start.12 = (bf16[96,320]{1,0:T(8,128)(2,1)S(1)}, bf16[96,320]{1,0:T(8,128)(2,1)S(1)}, u32[]{:S(2)}, u32[]{:S(2)}) collective-permute-start(bf16[96,320]{1,0:T(8,128)(2,1)S(1)} %bitcast.37), channel_id=1, source_target_pairs={{0,6},{2,0},{4,2},{6,4},{1,7},{3,1},{5,3},{7,5},{8,14},{10,8},{12,... | collective-permute-start | bytes 184328 | tf_op jit(solution)/shard_map/ppermute | solution.py:171
  112.9 4.8 %collective-permute-done.14.refs_15_ = bf16[8,1280,128]{2,1,0:T(8,128)(2,1)} collective-permute-done((bf16[8,1280,128]{2,1,0:T(8,128)(2,1)S(1)}, bf16[8,1280,128]{2,1,0:T(8,128)(2,1)}, u32[]{:S(2)}, u32[]{:S(2)}) %collective-permute-start.14) | collective-permute-done | bytes 2621472 | tf_op jit(solution)/shard_map/ppermute | solution.py:176
  124.0 15.8 %project.2.refs_1_.refs_16_ = f32[384,1920]{1,0:T(8,128)} custom-call(s32[5]{0:T(128)S(1)} %copy-done.31, bf16[96,5120]{1,0:T(8,128)(2,1)} %bitcast.8.refs_0_, bf16[96,5120]{1,0:T(8,128)(2,1)} %collective-permute-done.2.refs_3_.refs_1_, bf16[96,5120]{1,0:T(8,128)(2,1)S(1)} %copy-done.6, bf16[96,5120]{1,0:T(8,128)(2,1)} %collective-permute-done.8.refs_1_.refs_3_, ...), custom_call_target="tpu_custom_call" | custom-call | bytes 98304 | tf_op jit(solution)/shard_map/project/pallas_call | solution.py:423
  140.6 4.4 %collective-permute-done.18.refs_15_ = bf16[7,640,128]{2,1,0:T(8,128)(2,1)} collective-permute-done((bf16[7,640,128]{2,1,0:T(8,128)(2,1)}, bf16[7,640,128]{2,1,0:T(8,128)(2,1)}, u32[]{:S(2)}, u32[]{:S(2)}) %collective-permute-start.18) | collective-permute-done | bytes 1146912 | tf_op jit(solution)/shard_map/ppermute | solution.py:176
  145.9 8.3 %project.3 = (bf16[5,384,128]{2,1,0:T(8,128)(2,1)S(1)}, bf16[5,384,128]{2,1,0:T(8,128)(2,1)}, bf16[5,384,128]{2,1,0:T(8,128)(2,1)}, bf16[5,384,128]{2,1,0:T(8,128)(2,1)}, bf16[384,128]{1,0:T(8,128)(2,1)S(1)}) custom-call(s32[3]{0:T(128)S(1)} %add_add_fusion.1.order_ref, bf16[96,5120]{1,0:T(8,128)(2,1)} %bitcast.8.refs_0_, ...), custom_call_target="tpu_custom_call" | custom-call | bytes 98304 | tf_op jit(solution)/shard_map/project/pallas_call | solution.py:423
  156.6 2.6 collective-permute-start.21
  159.6 10.3 %collective-permute-done.19.refs_1_ = bf16[5,384,128]{2,1,0:T(8,128)(2,1)S(1)} collective-permute-done((bf16[5,384,128]{2,1,0:T(8,128)(2,1)}, bf16[5,384,128]{2,1,0:T(8,128)(2,1)S(1)}, u32[]{:S(2)}, u32[]{:S(2)}) %collective-permute-start.19) | collective-permute-done | bytes 491552 | tf_op jit(solution)/shard_map/ppermute | solution.py:176
  169.9 9.7 %collective-permute-done.20.refs_2_ = bf16[5,384,128]{2,1,0:T(8,128)(2,1)S(1)} collective-permute-done((bf16[5,384,128]{2,1,0:T(8,128)(2,1)}, bf16[5,384,128]{2,1,0:T(8,128)(2,1)S(1)}, u32[]{:S(2)}, u32[]{:S(2)}) %collective-permute-start.20) | collective-permute-done | bytes 491552 | tf_op jit(solution)/shard_map/ppermute | solution.py:176
  181.6 4.3 %attend.1 = (bf16[480,128]{1,0:T(8,128)(2,1)S(1)}, bf16[480,128]{1,0:T(8,128)(2,1)S(1)}, bf16[480,128]{1,0:T(8,128)(2,1)S(1)}, bf16[480,128]{1,0:T(8,128)(2,1)S(1)}) custom-call(s32[25]{0:T(128)S(1)} %pad_add_fusion.2.table_ref, bf16[5,384,128]{2,1,0:T(8,128)(2,1)S(1)} %copy-done.25, bf16[5,384,128]{2,1,0:T(8,128)(2,1)S(1)} %collective-permute-done.19.refs_1_, ...), custom_call_target="tpu_custom_call" | custom-call | bytes 98304 | tf_op jit(solution)/shard_map/attend/pallas_call | solution.py:480
  188.2 3.2 %collective-permute-start.23 = (bf16[480,128]{1,0:T(8,128)(2,1)S(1)}, bf16[480,128]{1,0:T(8,128)(2,1)S(1)}, u32[]{:S(2)}, u32[]{:S(2)}) collective-permute-start(bf16[480,128]{1,0:T(8,128)(2,1)S(1)} %get-tuple-element.25), channel_id=1, source_target_pairs={{0,4},{2,6},{4,0},{6,2},{1,5},{3,7},{5,1},{7,3},{8,12},{10,14},{12... | collective-permute-start | bytes 368648 | tf_op jit(solution)/shard_map/ppermute | solution.py:171
  191.4 3.7 %collective-permute-done.24 = bf16[480,128]{1,0:T(8,128)(2,1)S(1)} collective-permute-done((bf16[480,128]{1,0:T(8,128)(2,1)S(1)}, bf16[480,128]{1,0:T(8,128)(2,1)S(1)}, u32[]{:S(2)}, u32[]{:S(2)}) %collective-permute-start.24) | collective-permute-done | bytes 122912 | tf_op jit(solution)/shard_map/ppermute | solution.py:171
  195.1 5.0 %collective-permute-done.23 = bf16[480,128]{1,0:T(8,128)(2,1)S(1)} collective-permute-done((bf16[480,128]{1,0:T(8,128)(2,1)S(1)}, bf16[480,128]{1,0:T(8,128)(2,1)S(1)}, u32[]{:S(2)}, u32[]{:S(2)}) %collective-permute-start.23) | collective-permute-done | bytes 122912 | tf_op jit(solution)/shard_map/ppermute | solution.py:171
  203.1 11.2 %collective-permute-done.27.refs_2_ = bf16[4,480,128]{2,1,0:T(8,128)(2,1)S(1)} collective-permute-done((bf16[4,480,128]{2,1,0:T(8,128)(2,1)}, bf16[4,480,128]{2,1,0:T(8,128)(2,1)S(1)}, u32[]{:S(2)}, u32[]{:S(2)}) %collective-permute-start.27) | collective-permute-done | bytes 491552 | tf_op jit(solution)/shard_map/ppermute | solution.py:176
  219.6 3.5 %collective-permute-done.28.refs_3_ = bf16[2,480,128]{2,1,0:T(8,128)(2,1)S(1)} collective-permute-done((bf16[2,480,128]{2,1,0:T(8,128)(2,1)}, bf16[2,480,128]{2,1,0:T(8,128)(2,1)S(1)}, u32[]{:S(2)}, u32[]{:S(2)}) %collective-permute-start.28) | collective-permute-done | bytes 245792 | tf_op jit(solution)/shard_map/ppermute | solution.py:176
  223.0 3.1 %collective-permute-done.29.refs_4_ = bf16[2,480,128]{2,1,0:T(8,128)(2,1)} collective-permute-done((bf16[2,480,128]{2,1,0:T(8,128)(2,1)}, bf16[2,480,128]{2,1,0:T(8,128)(2,1)}, u32[]{:S(2)}, u32[]{:S(2)}) %collective-permute-start.29) | collective-permute-done | bytes 245792 | tf_op jit(solution)/shard_map/ppermute | solution.py:176
  229.2 8.4 %out_project.1 = (bf16[96,1280]{1,0:T(8,128)(2,1)S(1)}, bf16[96,1280]{1,0:T(8,128)(2,1)S(1)}, bf16[96,1280]{1,0:T(8,128)(2,1)S(1)}, bf16[96,1280]{1,0:T(8,128)(2,1)S(1)}) custom-call(s32[3]{0:T(128)S(1)} %add_add_fusion.at_ref, bf16[4,480,128]{2,1,0:T(8,128)(2,1)S(1)} %copy-done.10, bf16[4,480,128]{2,1,0:T(8,128)(2,1)S(1)} %copy-done.14, ...), custom_call_target="tpu_custom_call" | custom-call | bytes 983040 | tf_op jit(solution)/shard_map/out_project/pallas_call | solution.py:548
  241.9 5.0 %collective-permute-done.30.refs_1_ = bf16[96,1280]{1,0:T(8,128)(2,1)S(1)} collective-permute-done((bf16[96,1280]{1,0:T(8,128)(2,1)S(1)}, bf16[96,1280]{1,0:T(8,128)(2,1)S(1)}, u32[]{:S(2)}, u32[]{:S(2)}) %collective-permute-start.30) | collective-permute-done | bytes 245792 | tf_op jit(solution)/shard_map/ppermute | solution.py:176
  246.8 2.7 %collective-permute-done.31.refs_2_ = bf16[96,1280]{1,0:T(8,128)(2,1)S(1)} collective-permute-done((bf16[96,1280]{1,0:T(8,128)(2,1)S(1)}, bf16[96,1280]{1,0:T(8,128)(2,1)S(1)}, u32[]{:S(2)}, u32[]{:S(2)}) %collective-permute-start.31) | collective-permute-done | bytes 245792 | tf_op jit(solution)/shard_map/ppermute | solution.py:176
  (178 shorter events, 63.9 us)
Async XLA Ops:
  6.5 180.0 %all-gather.3.cloned.1.call-start = ((), (), s32[]{:S(2)}) async-start(), calls=%async_computation | async-start | bytes 4096000 | tf_op jit(solution)/shard_map/all_gather | solution.py:660
  9.9 36.6 %collective-permute-start = (bf16[8,1280,128]{2,1,0:T(8,128)(2,1)}, bf16[8,1280,128]{2,1,0:T(8,128)(2,1)S(1)}, u32[]{:S(2)}, u32[]{:S(2)}) collective-permute-start(bf16[8,1280,128]{2,1,0:T(8,128)(2,1)} %slice.25), channel_id=1, source_target_pairs={{0,8},{1,17},{8,0},{9,25},{16,24},{17,1},{24,16},{25,9},{2,10},{3,... | collective-permute-start | bytes 7864328 | tf_op jit(solution)/shard_map/ppermute | solution.py:606
  12.9 33.7 %collective-permute-start.2 = (bf16[96,5120]{1,0:T(8,128)(2,1)}, bf16[96,5120]{1,0:T(8,128)(2,1)}, u32[]{:S(2)}, u32[]{:S(2)}) collective-permute-start(bf16[96,5120]{1,0:T(8,128)(2,1)} %bitcast.8.refs_0_), channel_id=1, source_target_pairs={{0,2},{2,4},{4,6},{1,3},{3,5},{5,7},{8,10},{10,12},{12,14},{9,11},... | collective-permute-start | bytes 2949128 | tf_op jit(solution)/shard_map/ppermute | solution.py:181
  17.4 29.1 %collective-permute-start.3 = (bf16[96,5120]{1,0:T(8,128)(2,1)}, bf16[96,5120]{1,0:T(8,128)(2,1)}, u32[]{:S(2)}, u32[]{:S(2)}) collective-permute-start(bf16[96,5120]{1,0:T(8,128)(2,1)} %bitcast.8.refs_0_), channel_id=1, source_target_pairs={{2,0},{4,2},{6,4},{3,1},{5,3},{7,5},{10,8},{12,10},{14,12},{11,9},... | collective-permute-start | bytes 2949128 | tf_op jit(solution)/shard_map/ppermute | solution.py:182
  22.6 23.9 %collective-permute-start.1 = (bf16[2,4,48,256]{3,2,1,0:T(8,128)(2,1)}, bf16[2,4,48,256]{3,2,1,0:T(8,128)(2,1)S(1)}, u32[]{:S(2)}, u32[]{:S(2)}) collective-permute-start(bf16[2,4,48,256]{3,2,1,0:T(8,128)(2,1)} %after.12), channel_id=1, source_target_pairs={{0,8},{8,16},{16,24},{1,9},{9,17},{17,25},{2,10},{10,18},{18,26},{... | collective-permute-start | bytes 589832 | tf_op jit(solution)/shard_map/ppermute | solution.py:23
  48.7 38.5 %collective-permute-start.4 = (bf16[7,1280,128]{2,1,0:T(8,128)(2,1)}, bf16[7,1280,128]{2,1,0:T(8,128)(2,1)}, u32[]{:S(2)}, u32[]{:S(2)}) collective-permute-start(bf16[7,1280,128]{2,1,0:T(8,128)(2,1)} %after.13), channel_id=1, source_target_pairs={{0,8},{1,17},{8,0},{9,25},{16,24},{17,1},{24,16},{25,9},{2,10},{3,... | collective-permute-start | bytes 6881288 | tf_op jit(solution)/shard_map/ppermute | solution.py:614
  51.1 12.4 %collective-permute-start.5 = (bf16[96,5120]{1,0:T(8,128)(2,1)}, bf16[96,5120]{1,0:T(8,128)(2,1)S(1)}, u32[]{:S(2)}, u32[]{:S(2)}) collective-permute-start(bf16[96,5120]{1,0:T(8,128)(2,1)} %collective-permute-done.2.refs_3_.refs_1_), channel_id=1, source_target_pairs={{2,4},{4,6},{3,5},{5,7},{10,12},{12,14},{11,13},{13,15},{18,20},{2... | collective-permute-start | bytes 2949128 | tf_op jit(solution)/shard_map/ppermute | solution.py:181
  51.8 23.8 %collective-permute-start.7 = (bf16[96,5120]{1,0:T(8,128)(2,1)}, bf16[96,5120]{1,0:T(8,128)(2,1)S(1)}, u32[]{:S(2)}, u32[]{:S(2)}) collective-permute-start(bf16[96,5120]{1,0:T(8,128)(2,1)} %collective-permute-done.3.refs_4_), channel_id=1, source_target_pairs={{2,0},{4,2},{3,1},{5,3},{10,8},{12,10},{11,9},{13,11},{18,16},{20,... | collective-permute-start | bytes 2949128 | tf_op jit(solution)/shard_map/ppermute | solution.py:182
  54.4 9.1 %collective-permute-start.6 = (bf16[4,1,48,256]{3,2,1,0:T(8,128)(2,1)S(1)}, bf16[4,1,48,256]{3,2,1,0:T(8,128)(2,1)S(1)}, u32[]{:S(2)}, u32[]{:S(2)}) collective-permute-start(bf16[4,1,48,256]{3,2,1,0:T(8,128)(2,1)S(1)} %slice.26), channel_id=1, source_target_pairs={{0,2},{2,4},{4,6},{1,3},{3,5},{5,7},{8,10},{10,12},{12,14},{9,11},... | collective-permute-start | bytes 294920 | tf_op jit(solution)/shard_map/ppermute | solution.py:23
  65.1 41.8 %collective-permute-start.8 = (bf16[96,5120]{1,0:T(8,128)(2,1)}, bf16[96,5120]{1,0:T(8,128)(2,1)}, u32[]{:S(2)}, u32[]{:S(2)}) collective-permute-start(bf16[96,5120]{1,0:T(8,128)(2,1)} %after.14.refs_1_.refs_2_), channel_id=1, source_target_pairs={{4,6},{5,7},{12,14},{13,15},{20,22},{21,23},{28,30},{29,31}} | collective-permute-start | bytes 2949128 | tf_op jit(solution)/shard_map/ppermute | solution.py:181
  76.6 30.4 %collective-permute-start.9 = (bf16[96,5120]{1,0:T(8,128)(2,1)}, bf16[96,5120]{1,0:T(8,128)(2,1)}, u32[]{:S(2)}, u32[]{:S(2)}) collective-permute-start(bf16[96,5120]{1,0:T(8,128)(2,1)} %after.15.refs_2_.refs_5_), channel_id=1, source_target_pairs={{2,0},{3,1},{10,8},{11,9},{18,16},{19,17},{26,24},{27,25}} | collective-permute-start | bytes 2949128 | tf_op jit(solution)/shard_map/ppermute | solution.py:182
  96.0 11.0 %collective-permute-start.10 = (bf16[96,320]{1,0:T(8,128)(2,1)S(1)}, bf16[96,320]{1,0:T(8,128)(2,1)S(1)}, u32[]{:S(2)}, u32[]{:S(2)}) collective-permute-start(bf16[96,320]{1,0:T(8,128)(2,1)S(1)} %bitcast.35), channel_id=1, source_target_pairs={{0,2},{2,4},{4,6},{6,0},{1,3},{3,5},{5,7},{7,1},{8,10},{10,12},{12... | collective-permute-start | bytes 184328 | tf_op jit(solution)/shard_map/ppermute | solution.py:171
  99.9 7.1 %collective-permute-start.11 = (bf16[96,320]{1,0:T(8,128)(2,1)S(1)}, bf16[96,320]{1,0:T(8,128)(2,1)S(1)}, u32[]{:S(2)}, u32[]{:S(2)}) collective-permute-start(bf16[96,320]{1,0:T(8,128)(2,1)S(1)} %bitcast.36), channel_id=1, source_target_pairs={{0,4},{2,6},{4,0},{6,2},{1,5},{3,7},{5,1},{7,3},{8,12},{10,14},{12... | collective-permute-start | bytes 184328 | tf_op jit(solution)/shard_map/ppermute | solution.py:171
  109.6 8.1 %collective-permute-start.14 = (bf16[8,1280,128]{2,1,0:T(8,128)(2,1)S(1)}, bf16[8,1280,128]{2,1,0:T(8,128)(2,1)}, u32[]{:S(2)}, u32[]{:S(2)}) collective-permute-start(bf16[8,1280,128]{2,1,0:T(8,128)(2,1)S(1)} %copy-done.1), channel_id=1, source_target_pairs={{0,1},{1,0},{2,3},{3,2},{4,5},{5,4},{6,7},{7,6},{8,9},{9,8},{10,11... | collective-permute-start | bytes 7864328 | tf_op jit(solution)/shard_map/ppermute | solution.py:176
  109.7 8.5 %collective-permute-start.15 = (bf16[7,1280,128]{2,1,0:T(8,128)(2,1)}, bf16[7,1280,128]{2,1,0:T(8,128)(2,1)}, u32[]{:S(2)}, u32[]{:S(2)}) collective-permute-start(bf16[7,1280,128]{2,1,0:T(8,128)(2,1)} %after.16.refs_14_), channel_id=1, source_target_pairs={{0,1},{1,0},{2,3},{3,2},{4,5},{5,4},{6,7},{7,6},{8,9},{9,8},{10,11... | collective-permute-start | bytes 6881288 | tf_op jit(solution)/shard_map/ppermute | solution.py:176
  110.2 29.7 %collective-permute-start.13 = (bf16[8,640,128]{2,1,0:T(8,128)(2,1)}, bf16[8,640,128]{2,1,0:T(8,128)(2,1)}, u32[]{:S(2)}, u32[]{:S(2)}) collective-permute-start(bf16[8,640,128]{2,1,0:T(8,128)(2,1)} %constant_dynamic-slice_fusion.1.refs_3_), channel_id=1, source_target_pairs={{0,16},{1,9},{8,24},{9,1},{16,0},{17,25},{24,8},{25,17},{2,18},{3,... | collective-permute-start | bytes 3932168 | tf_op jit(solution)/shard_map/ppermute | solution.py:634
  110.5 29.9 %collective-permute-start.16 = (bf16[7,640,128]{2,1,0:T(8,128)(2,1)}, bf16[7,640,128]{2,1,0:T(8,128)(2,1)}, u32[]{:S(2)}, u32[]{:S(2)}) collective-permute-start(bf16[7,640,128]{2,1,0:T(8,128)(2,1)} %constant_dynamic-slice_fusion.refs_1_), channel_id=1, source_target_pairs={{0,16},{1,9},{8,24},{9,1},{16,0},{17,25},{24,8},{25,17},{2,18},{3,... | collective-permute-start | bytes 3440648 | tf_op jit(solution)/shard_map/ppermute | solution.py:634
  139.9 5.1 %collective-permute-start.17 = (bf16[8,640,128]{2,1,0:T(8,128)(2,1)}, bf16[8,640,128]{2,1,0:T(8,128)(2,1)S(1)}, u32[]{:S(2)}, u32[]{:S(2)}) collective-permute-start(bf16[8,640,128]{2,1,0:T(8,128)(2,1)} %after.20.refs_12_), channel_id=1, source_target_pairs={{0,1},{1,0},{2,3},{3,2},{4,5},{5,4},{6,7},{7,6},{8,9},{9,8},{10,11... | collective-permute-start | bytes 3932168 | tf_op jit(solution)/shard_map/ppermute | solution.py:176
  155.6 14.3 %collective-permute-start.19 = (bf16[5,384,128]{2,1,0:T(8,128)(2,1)}, bf16[5,384,128]{2,1,0:T(8,128)(2,1)S(1)}, u32[]{:S(2)}, u32[]{:S(2)}) collective-permute-start(bf16[5,384,128]{2,1,0:T(8,128)(2,1)} %get-tuple-element.19), channel_id=1, source_target_pairs={{0,8},{8,0},{16,24},{24,16},{1,9},{9,1},{17,25},{25,17},{2,10},{10... | collective-permute-start | bytes 1474568 | tf_op jit(solution)/shard_map/ppermute | solution.py:176
  155.6 24.0 %collective-permute-start.20 = (bf16[5,384,128]{2,1,0:T(8,128)(2,1)}, bf16[5,384,128]{2,1,0:T(8,128)(2,1)S(1)}, u32[]{:S(2)}, u32[]{:S(2)}) collective-permute-start(bf16[5,384,128]{2,1,0:T(8,128)(2,1)} %get-tuple-element.20), channel_id=1, source_target_pairs={{0,16},{8,24},{16,0},{24,8},{1,17},{9,25},{17,1},{25,9},{2,18},{10... | collective-permute-start | bytes 1474568 | tf_op jit(solution)/shard_map/ppermute | solution.py:176
  156.6 23.1 %collective-permute-start.21 = (bf16[5,384,128]{2,1,0:T(8,128)(2,1)}, bf16[5,384,128]{2,1,0:T(8,128)(2,1)S(1)}, u32[]{:S(2)}, u32[]{:S(2)}) collective-permute-start(bf16[5,384,128]{2,1,0:T(8,128)(2,1)} %get-tuple-element.21), channel_id=1, source_target_pairs={{0,24},{8,16},{16,8},{24,0},{1,25},{9,17},{17,9},{25,1},{2,26},{10... | collective-permute-start | bytes 1474568 | tf_op jit(solution)/shard_map/ppermute | solution.py:176
  186.6 14.3 %collective-permute-start.25 = (bf16[4,640,640]{2,1,0:T(8,128)(2,1)}, bf16[4,640,640]{2,1,0:T(8,128)(2,1)}, u32[]{:S(2)}, u32[]{:S(2)}) collective-permute-start(bf16[4,640,640]{2,1,0:T(8,128)(2,1)} %after.22.refs_5_), channel_id=1, source_target_pairs={{0,1},{1,0},{2,3},{3,2},{4,5},{5,4},{6,7},{7,6},{8,9},{9,8},{10,11... | collective-permute-start | bytes 9830408 | tf_op jit(solution)/shard_map/ppermute | solution.py:176
  186.6 8.5 %collective-permute-start.24 = (bf16[480,128]{1,0:T(8,128)(2,1)S(1)}, bf16[480,128]{1,0:T(8,128)(2,1)S(1)}, u32[]{:S(2)}, u32[]{:S(2)}) collective-permute-start(bf16[480,128]{1,0:T(8,128)(2,1)S(1)} %get-tuple-element.26), channel_id=1, source_target_pairs={{0,2},{2,4},{4,6},{6,0},{1,3},{3,5},{5,7},{7,1},{8,10},{10,12},{12... | collective-permute-start | bytes 368648 | tf_op jit(solution)/shard_map/ppermute | solution.py:171
  188.2 11.9 %collective-permute-start.23 = (bf16[480,128]{1,0:T(8,128)(2,1)S(1)}, bf16[480,128]{1,0:T(8,128)(2,1)S(1)}, u32[]{:S(2)}, u32[]{:S(2)}) collective-permute-start(bf16[480,128]{1,0:T(8,128)(2,1)S(1)} %get-tuple-element.25), channel_id=1, source_target_pairs={{0,4},{2,6},{4,0},{6,2},{1,5},{3,7},{5,1},{7,3},{8,12},{10,14},{12... | collective-permute-start | bytes 368648 | tf_op jit(solution)/shard_map/ppermute | solution.py:171
  191.4 8.7 %collective-permute-start.22 = (bf16[480,128]{1,0:T(8,128)(2,1)S(1)}, bf16[480,128]{1,0:T(8,128)(2,1)S(1)}, u32[]{:S(2)}, u32[]{:S(2)}) collective-permute-start(bf16[480,128]{1,0:T(8,128)(2,1)S(1)} %get-tuple-element.24), channel_id=1, source_target_pairs={{0,6},{2,0},{4,2},{6,4},{1,7},{3,1},{5,3},{7,5},{8,14},{10,8},{12,... | collective-permute-start | bytes 368648 | tf_op jit(solution)/shard_map/ppermute | solution.py:171
  200.9 13.4 %collective-permute-start.27 = (bf16[4,480,128]{2,1,0:T(8,128)(2,1)}, bf16[4,480,128]{2,1,0:T(8,128)(2,1)S(1)}, u32[]{:S(2)}, u32[]{:S(2)}) collective-permute-start(bf16[4,480,128]{2,1,0:T(8,128)(2,1)} %after.23.refs_0_), channel_id=1, source_target_pairs={{0,16},{8,24},{16,0},{24,8},{1,17},{9,25},{17,1},{25,9},{2,18},{10... | collective-permute-start | bytes 1474568 | tf_op jit(solution)/shard_map/ppermute | solution.py:176
  202.4 15.2 %collective-permute-start.26 = (bf16[4,480,128]{2,1,0:T(8,128)(2,1)}, bf16[4,480,128]{2,1,0:T(8,128)(2,1)S(1)}, u32[]{:S(2)}, u32[]{:S(2)}) collective-permute-start(bf16[4,480,128]{2,1,0:T(8,128)(2,1)} %after.23.refs_0_), channel_id=1, source_target_pairs={{0,8},{8,0},{16,24},{24,16},{1,9},{9,1},{17,25},{25,17},{2,10},{10... | collective-permute-start | bytes 1474568 | tf_op jit(solution)/shard_map/ppermute | solution.py:176
  215.8 7.3 %collective-permute-start.28 = (bf16[2,480,128]{2,1,0:T(8,128)(2,1)}, bf16[2,480,128]{2,1,0:T(8,128)(2,1)S(1)}, u32[]{:S(2)}, u32[]{:S(2)}) collective-permute-start(bf16[2,480,128]{2,1,0:T(8,128)(2,1)} %slice.28), channel_id=1, source_target_pairs={{0,8},{8,0},{16,24},{24,16},{1,9},{9,1},{17,25},{25,17},{2,10},{10... | collective-permute-start | bytes 737288 | tf_op jit(solution)/shard_map/ppermute | solution.py:176
  219.1 7.1 %collective-permute-start.29 = (bf16[2,480,128]{2,1,0:T(8,128)(2,1)}, bf16[2,480,128]{2,1,0:T(8,128)(2,1)}, u32[]{:S(2)}, u32[]{:S(2)}) collective-permute-start(bf16[2,480,128]{2,1,0:T(8,128)(2,1)} %slice.29), channel_id=1, source_target_pairs={{0,16},{8,24},{16,0},{24,8},{1,17},{9,25},{17,1},{25,9},{2,18},{10... | collective-permute-start | bytes 737288 | tf_op jit(solution)/shard_map/ppermute | solution.py:176
  238.4 8.5 %collective-permute-start.30 = (bf16[96,1280]{1,0:T(8,128)(2,1)S(1)}, bf16[96,1280]{1,0:T(8,128)(2,1)S(1)}, u32[]{:S(2)}, u32[]{:S(2)}) collective-permute-start(bf16[96,1280]{1,0:T(8,128)(2,1)S(1)} %get-tuple-element.28), channel_id=1, source_target_pairs={{0,8},{8,0},{16,24},{24,16},{1,9},{9,1},{17,25},{25,17},{2,10},{10... | collective-permute-start | bytes 737288 | tf_op jit(solution)/shard_map/ppermute | solution.py:176
  238.6 10.9 %collective-permute-start.31 = (bf16[96,1280]{1,0:T(8,128)(2,1)S(1)}, bf16[96,1280]{1,0:T(8,128)(2,1)S(1)}, u32[]{:S(2)}, u32[]{:S(2)}) collective-permute-start(bf16[96,1280]{1,0:T(8,128)(2,1)S(1)} %get-tuple-element.29), channel_id=1, source_target_pairs={{0,16},{8,24},{16,0},{24,8},{1,17},{9,25},{17,1},{25,9},{2,18},{10... | collective-permute-start | bytes 737288 | tf_op jit(solution)/shard_map/ppermute | solution.py:176
  240.1 9.4 %collective-permute-start.32 = (bf16[96,1280]{1,0:T(8,128)(2,1)S(1)}, bf16[96,1280]{1,0:T(8,128)(2,1)S(1)}, u32[]{:S(2)}, u32[]{:S(2)}) collective-permute-start(bf16[96,1280]{1,0:T(8,128)(2,1)S(1)} %get-tuple-element.30), channel_id=1, source_target_pairs={{0,24},{8,16},{16,8},{24,0},{1,25},{9,17},{17,9},{25,1},{2,26},{10... | collective-permute-start | bytes 737288 | tf_op jit(solution)/shard_map/ppermute | solution.py:176
  (46 other events, 210.5 us)
Sparse Core Ops, SparseCore 0:
  109.7 65.5 all-gather.2
